TPU v7x, 256 devices: a whole 4x4x8 slice. The times are simulated.
256 devices in a mesh: ctx: 32 (over y, x, z_hi), head: 8 (over z_lo, core).
Axes of the slice: x: 4, y: 4, z: 8 (z_hi: 2, z_lo: 4; z = z_hi * 4 + z_lo), core: 2. Of those that a mesh axis runs over, the one named last changes fastest.
Arguments:
- queries: bfloat16 [16384, 3072], P(('ctx', 'head')), may hold values from -200 to 200
- keys: bfloat16 [16384, 3072], P(('ctx', 'head')), may hold values from -18 to 18
- values: bfloat16 [16384, 3072], P(('ctx', 'head')), may hold values from -6 to 6
- residual: bfloat16 [16384, 3072], P(('ctx', 'head')), may hold values from -6 to 6
- out_weight: bfloat16 [3072, 3072], P('head'), may hold values from -0.4375 to 0.4375
- gate_table: float32 [8, 3072], replicated, may hold values from 0.3 to 3
- span_lengths: int32 [4], replicated, may hold values from 1 to 8192, 16384 in all
- noise_levels: int32 [4], replicated, may hold values from 0 to 7
Outputs:
- mixed: bfloat16 [16384, 3072], P(('ctx', 'head'))
Inputs may be any that keep to these rules, and one draw needn't show every extreme that they name: `span_lengths`: 4 positive lengths that sum to 16384; the largest is 8192.
All inputs are finite; a program needn't handle non-finite values.
Results may differ from a plain program's by a relative error of at most 0.024.
Values may be sent and summed in bfloat16 or wider, within the bound.
No kernel may reach another device: no remote copies, remote signals or barrier semaphores. Data moves between devices by JAX's collectives and lax.ppermute only.
A program may use at most 192 MiB of HBM per device.

v0:
```python
import jax
import jax.numpy as jnp
from jax import lax
from jax.sharding import PartitionSpec as P

HEAD_DIM = 128


def spans_at(ends, first, count):
    positions = first + jnp.arange(count, dtype=jnp.int32)
    return jnp.sum((positions[:, None] >= ends[None, :]).astype(jnp.int32), axis=1)


def local(queries, keys, values, residual, out_weight, gate_table, span_lengths, noise_levels):
    scale = HEAD_DIM ** (-0.5)
    head_q, head_k, head_v = (
        lax.all_to_all(queries, "head", split_axis=1, concat_axis=0, tiled=True),
        lax.all_to_all(keys, "head", split_axis=1, concat_axis=0, tiled=True),
        lax.all_to_all(values, "head", split_axis=1, concat_axis=0, tiled=True),
    )
    rows = head_q.shape[0]
    per_dev = head_q.shape[1] // HEAD_DIM
    ctx_pos = lax.axis_index("ctx")
    ends = jnp.cumsum(span_lengths)
    my_span = spans_at(ends, ctx_pos * rows, rows)
    q_rows = head_q.reshape(rows, per_dev, HEAD_DIM)
    start_state = (
        jnp.full((rows, per_dev), -1e30, jnp.float32),
        jnp.zeros((rows, per_dev), jnp.float32),
        jnp.zeros((rows, per_dev, HEAD_DIM), jnp.float32),
    )
    piece_k = lax.all_gather(head_k, "ctx", axis=0, tiled=True)
    piece_v = lax.all_gather(head_v, "ctx", axis=0, tiled=True)
    count = piece_k.shape[0]
    stride = 512
    steps_in = count // stride
    k_parts = piece_k.reshape(steps_in, stride, per_dev, HEAD_DIM)
    v_parts = piece_v.reshape(steps_in, stride, per_dev, HEAD_DIM)

    def one_part(state, inner):
        k_blk, v_blk, index = inner
        key_span = spans_at(ends, index * stride, stride)
        peak_old, total_old, summed_old = state
        scores = (
            jnp.einsum("qhd,khd->qhk", q_rows, k_blk, preferred_element_type=jnp.float32) * scale
        )
        visible = key_span[None, None, :] <= my_span[:, None, None]
        peak_new = jnp.maximum(peak_old, jnp.max(jnp.where(visible, scores, -1e30), axis=2))
        weight = jnp.where(visible, jnp.exp(scores - peak_new[:, :, None]), 0.0)
        fade = jnp.exp(peak_old - peak_new)
        total_new = total_old * fade + jnp.sum(weight, axis=2)
        summed_new = summed_old * fade[:, :, None] + jnp.einsum(
            "qhk,khd->qhd", weight.astype(jnp.bfloat16), v_blk, preferred_element_type=jnp.float32
        )
        return ((peak_new, total_new, summed_new), None)

    result, unused = lax.scan(
        one_part, start_state, (k_parts, v_parts, jnp.arange(steps_in, dtype=jnp.int32))
    )
    peak, total, summed = result
    attn = (summed / total[:, :, None]).reshape(rows, per_dev * HEAD_DIM).astype(jnp.bfloat16)
    mine = rows // lax.axis_size("head")
    proj = lax.psum_scatter(
        jnp.dot(attn, out_weight, preferred_element_type=jnp.float32).astype(jnp.bfloat16),
        "head",
        scatter_dimension=0,
        tiled=True,
    ).astype(jnp.float32)
    tok_span = spans_at(ends, ctx_pos * rows + lax.axis_index("head") * mine, mine)
    span_ids = jnp.arange(span_lengths.shape[0], dtype=jnp.int32)
    tok_level = jnp.sum(
        jnp.where(tok_span[:, None] == span_ids[None, :], noise_levels[None, :], 0), axis=1
    )
    level_ids = jnp.arange(gate_table.shape[0], dtype=jnp.int32)
    one_hot = (tok_level[:, None] == level_ids[None, :]).astype(jnp.float32)
    gate = jnp.dot(one_hot, gate_table, precision=lax.Precision.HIGHEST)
    return (residual.astype(jnp.float32) + gate * proj).astype(jnp.bfloat16)


def solution(mesh):
    return jax.shard_map(
        local,
        mesh=mesh,
        in_specs=(
            P(("ctx", "head"), None),
            P(("ctx", "head"), None),
            P(("ctx", "head"), None),
            P(("ctx", "head"), None),
            P("head", None),
            P(),
            P(),
            P(),
        ),
        out_specs=P(("ctx", "head"), None),
        check_vma=False,
    )
```

profile of v0, /device:TPU:2, one launch (start us, length us, event | category | flops | bytes accessed | tf_op | source)
XLA Modules:
  0.0 880.2 jit_solution(14187120984498073333)
XLA Ops:
  7.7 18.4 %all_to_all.54 = bf16[64,8,384]{2,0,1:T(8,128)(2,1)} all-to-all(bf16[64,8,384]{2,0,1:T(8,128)(2,1)S(1)} %bitcast.76), channel_id=1, replica_groups=mesh['ctx'=32,'head'=8] {'head'}, dimensions={1} | all-to-all | bytes 786432 | tf_op jit(solution)/shard_map/all_to_all | solution.py:18
  27.2 15.6 %all_to_all.55 = bf16[64,8,384]{2,0,1:T(8,128)(2,1)} all-to-all(bf16[64,8,384]{2,0,1:T(8,128)(2,1)S(1)} %bitcast.77), channel_id=1, replica_groups=mesh['ctx'=32,'head'=8] {'head'}, dimensions={1} | all-to-all | bytes 786432 | tf_op jit(solution)/shard_map/all_to_all | solution.py:19
  43.7 3.5 all-to-all-start.1
  48.1 12.1 %all-to-all-done.1 = bf16[64,8,384]{2,0,1:T(8,128)(2,1)S(1)} async-done(((bf16[64,8,384]{2,0,1:T(8,128)(2,1)}), bf16[64,8,384]{2,0,1:T(8,128)(2,1)S(1)}, u32[]{:S(2)}, u32[]{:S(2)}) %all-to-all-start.1) | async-done | bytes 393248 | tf_op jit(solution)/shard_map/all_to_all | solution.py:17
  60.4 165.7 %all-gather.3.cloned.1.call-done = bf16[16384,384]{1,0:T(8,128)(2,1)} async-done(((bf16[512,384]{1,0:T(8,128)(2,1)}), bf16[16384,384]{1,0:T(8,128)(2,1)}) %all-gather.3.cloned.1.call-update) | async-done | bytes 12582928 | tf_op jit(solution)/shard_map/all_gather | solution.py:32
  226.1 32.2 %reshape.98 = bf16[32,512,3,128]{3,2,1,0:T(4,128)(2,1)} reshape(bf16[16384,384]{1,0:T(8,128)(2,1)} %all-gather.3.cloned.1.call-done) | data formatting | bytes 25165824 | tf_op jit(solution)/shard_map/reshape | solution.py:37
  258.3 13.0 %copy.41 = bf16[32,512,3,128]{3,1,2,0:T(8,128)(2,1)} copy(bf16[32,512,3,128]{3,2,1,0:T(4,128)(2,1)} %reshape.98) | data formatting | bytes 25165824
  271.3 152.2 %all-gather.5.cloned.1.call-done = bf16[16384,384]{1,0:T(8,128)(2,1)} async-done(((bf16[512,384]{1,0:T(8,128)(2,1)}), bf16[16384,384]{1,0:T(8,128)(2,1)}) %all-gather.5.cloned.1.call-update) | async-done | bytes 12582928 | tf_op jit(solution)/shard_map/all_gather | solution.py:33
  423.5 32.1 %reshape.99 = bf16[32,512,3,128]{3,2,1,0:T(4,128)(2,1)} reshape(bf16[16384,384]{1,0:T(8,128)(2,1)} %all-gather.5.cloned.1.call-done) | data formatting | bytes 25165824 | tf_op jit(solution)/shard_map/reshape | solution.py:38
  455.7 24.8 %copy.43 = bf16[32,512,3,128]{1,3,2,0:T(8,128)(2,1)} copy(bf16[32,512,3,128]{3,2,1,0:T(4,128)(2,1)} %reshape.99) | data formatting | bytes 25165824
  480.5 345.8 %while.15 = (s32[]{:T(128)}, f32[512,3]{0,1:T(4,128)S(1)}, f32[512,3]{0,1:T(4,128)S(1)}, f32[512,3,128]{0,2,1:T(8,128)}, s32[32]{0:T(128)S(1)}, /*index=5*/s32[4...) while((s32[]{:T(128)}, f32[512,3]{0,1:T(4,128)S(1)}, ...), condition=%wide.region_8.9_spmd.clone, body=%wide.region_4.8_spmd.clone.sunk | while | flops 412169728 | bytes 25930960 | solution.py:57
  482.0 3.4 fusion.44
  492.6 3.4 fusion.44
  498.8 3.1 fusion.47
  503.4 3.4 fusion.44
  509.6 3.1 fusion.47
  514.2 3.4 fusion.44
  520.4 3.1 fusion.47
  525.0 3.4 fusion.44
  535.9 3.4 fusion.44
  546.7 3.4 fusion.44
  557.5 3.4 fusion.44
  568.3 3.4 fusion.44
  579.1 3.4 fusion.44
  589.9 3.4 fusion.44
  600.7 3.4 fusion.44
  611.5 3.4 fusion.44
  622.4 3.4 fusion.44
  633.2 3.4 fusion.44
  644.0 3.4 fusion.44
  654.8 3.4 fusion.44
  665.6 3.4 fusion.44
  676.4 3.4 fusion.44
  687.2 3.4 fusion.44
  698.0 3.4 fusion.44
  708.9 3.4 fusion.44
  719.7 3.4 fusion.44
  730.5 3.4 fusion.44
  741.3 3.4 fusion.44
  752.1 3.4 fusion.44
  762.9 3.4 fusion.44
  773.7 3.4 fusion.44
  784.5 3.4 fusion.44
  795.4 3.4 fusion.44
  806.2 3.4 fusion.44
  817.0 3.4 fusion.44
  827.5 3.5 convolution_convert_fusion
  831.2 40.2 %reduce-scatter.2.cloned.1.call-done = bf16[64,3072]{1,0:T(8,128)(2,1)} async-done(((bf16[512,3072]{1,0:T(8,128)(2,1)}), bf16[64,3072]{1,0:T(8,128)(2,1)}) %reduce-scatter.2.cloned.1.call-update) | async-done | bytes 393232 | tf_op jit(solution)/shard_map/reduce_scatter | solution.py:63
  (390 shorter events, 215.2 us)
Async XLA Ops:
  6.5 820.9 %copy-start = (bf16[384,3072]{1,0:T(8,128)(2,1)S(1)}, bf16[384,3072]{1,0:T(8,128)(2,1)}, u32[]{:S(2)}) copy-start(bf16[384,3072]{1,0:T(8,128)(2,1)} %param.14) | copy-start | bytes 7077892
  6.5 36.4 %copy-start.2 = (bf16[64,3072]{1,0:T(8,128)(2,1)S(1)}, bf16[64,3072]{1,0:T(8,128)(2,1)}, u32[]{:S(2)}) copy-start(bf16[64,3072]{1,0:T(8,128)(2,1)} %param.10) | copy-start | bytes 1179652
  6.5 40.7 %copy-start.8 = (s32[4]{0:T(128)S(1)}, s32[4]{0:T(128)}, u32[]{:S(2)}) copy-start(s32[4]{0:T(128)} %param.16) | copy-start | bytes 52
  6.5 219.6 %all-gather.3.cloned.1.call-start = ((), (), s32[]{:S(2)}) async-start(), calls=%async_computation.4 | async-start | bytes 12976128 | tf_op jit(solution)/shard_map/all_gather | solution.py:32
  26.1 397.4 %all-gather.5.cloned.1.call-start = ((), (), s32[]{:S(2)}) async-start(), calls=%async_computation.5 | async-start | bytes 12976128 | tf_op jit(solution)/shard_map/all_gather | solution.py:33
  43.7 16.5 %all-to-all-start.1 = ((bf16[64,8,384]{2,0,1:T(8,128)(2,1)}), bf16[64,8,384]{2,0,1:T(8,128)(2,1)S(1)}, u32[]{:S(2)}, u32[]{:S(2)}) async-start(bf16[64,8,384]{2,0,1:T(8,128)(2,1)} %bitcast.55), calls=%async_computation.1 | async-start | bytes 786432 | tf_op jit(solution)/shard_map/all_to_all | solution.py:17
  47.2 824.2 %reduce-scatter.2.cloned.1.call-start = ((), (), s32[]{:S(2)}) async-start(), calls=%async_computation.6 | async-start | bytes 3538944 | tf_op jit(solution)/shard_map/reduce_scatter | solution.py:63
  47.4 12.8 %copy-start.6 = (s32[4,1]{0,1:T(1,128)}, s32[4,1]{0,1:T(1,128)S(1)}, u32[]{:S(2)}) copy-start(s32[4,1]{0,1:T(1,128)S(1)} %reduce-window.8) | copy-start | bytes 52
  455.6 24.8 %copy-start.5 = (s32[512]{0:T(512)S(1)}, s32[512]{0:T(512)}, u32[]{:S(2)}) copy-start(s32[512]{0:T(512)} %convert_reduce_fusion.1) | copy-start | bytes 6148
  455.7 24.8 %copy-start.7 = (s32[4,1]{0,1:T(1,128)S(1)}, s32[4,1]{0,1:T(1,128)}, u32[]{:S(2)}) copy-start(s32[4,1]{0,1:T(1,128)} %copy-done.6) | copy-start | bytes 52
  485.4 2.8 copy-start.1
  496.0 2.8 copy-start.1
  506.8 2.8 copy-start.1
  517.6 2.8 copy-start.1
  528.4 2.8 copy-start.1
  539.2 2.8 copy-start.1
  550.0 2.8 copy-start.1
  560.8 2.8 copy-start.1
  571.7 2.8 copy-start.1
  582.5 2.8 copy-start.1
  593.3 2.8 copy-start.1
  604.1 2.8 copy-start.1
  614.9 2.8 copy-start.1
  625.7 2.8 copy-start.1
  636.5 2.8 copy-start.1
  647.3 2.8 copy-start.1
  658.2 2.8 copy-start.1
  669.0 2.8 copy-start.1
  679.8 2.8 copy-start.1
  690.6 2.8 copy-start.1
  701.4 2.8 copy-start.1
  712.2 2.8 copy-start.1
  723.0 2.8 copy-start.1
  733.8 2.8 copy-start.1
  744.7 2.8 copy-start.1
  755.5 2.8 copy-start.1
  766.3 2.8 copy-start.1
  777.1 2.8 copy-start.1
  787.9 2.8 copy-start.1
  798.7 2.8 copy-start.1
  809.5 2.8 copy-start.1
  820.3 2.8 copy-start.1
  827.5 3.7 copy-start.9
  827.5 43.9 %copy-start.3 = (bf16[64,3072]{1,0:T(8,128)(2,1)S(1)}, bf16[64,3072]{1,0:T(8,128)(2,1)}, u32[]{:S(2)}) copy-start(bf16[64,3072]{1,0:T(8,128)(2,1)} %param.13) | copy-start | bytes 1179652
  827.5 43.9 %copy-start.4 = (f32[8,3072]{1,0:T(8,128)S(1)}, f32[8,3072]{1,0:T(8,128)}, u32[]{:S(2)}) copy-start(f32[8,3072]{1,0:T(8,128)} %param.15) | copy-start | bytes 294916
Sparse Core Ops, SparseCore 0:
  26.2 199.8 all-gather.2
  229.6 193.8 all-gather.4
  831.2 40.1 reduce-scatter.1
where the time goes:
time: 885 us; the launch traced here: 880 us
  waiting for transfers between devices  370 us (42%)
  matrix products  211 us (24%)
  local copies, waits for them, and re-layouts  126 us (14%)
  other arithmetic  101 us (11%)
  blocking collectives  34 us (4%)
  loops' own time  21.7 us (2%)
  between operations  13.3 us (2%)
    all_gather x1, waiting for transfers between devices, local(): piece_k = lax.all_gather(head_k, 'ctx', axis=0, tiled=True)  166 us
    all_gather x1, waiting for transfers between devices, local(): piece_v = lax.all_gather(head_v, 'ctx', axis=0, tiled=True)  152 us
    dot_general x32, matrix products, one_part(): jnp.einsum('qhd,khd->qhk', q_rows, k_blk, preferred_element_type=jnp.floa...  108 us
    dot_general x32, matrix products, one_part(): jnp.einsum('qhk,khd->qhd', weight.astype(jnp.bfloat16), v_blk, preferred_...  97.5 us
    reduce_sum x32, other arithmetic, one_part(): total_new = total_old * fade + jnp.sum(weight, axis=2)  87.7 us
    reduce_scatter x1, waiting for transfers between devices, local(): lax.psum_scatter(jnp.dot(attn, out_weight, preferred_element_type=jnp.flo...  40.2 us
    unnamed x21, local copies, waits for them, and re-layouts  37.9 us
    reshape x1, local copies, waits for them, and re-layouts, local(): k_parts = piece_k.reshape(steps_in, stride, per_dev, HEAD_DIM)  32.2 us
  transfers between devices with their start and end apart: 4, of which 4 were waited for; matrix products, arithmetic and copies ran while one was open for 5% of the time, Pallas kernels for 0%

commit v1 on v0

v1 whole, which is shorter than its diff:
```python
import jax
import jax.numpy as jnp
from jax import lax
from jax.sharding import Mesh, PartitionSpec as P
from jax.experimental import pallas as pl
from jax.experimental.pallas import tpu as pltpu

HD = 128
PER = 3
W = PER * HD
TOK = 64
SCALE2 = HD ** (-0.5) * 1.4426950408889634
NEG = -1e30
NY, NX, NZ, NC = 4, 4, 8, 2
QT = 256
KT = 512
ROWS = TOK + 8


def attention_kernel(ends_ref, pos_ref, *refs):
    q_in = refs[0:4]
    kv_in = refs[4:14]
    o_ref, lse_ref = refs[14:16]
    q_s, kv_s, qt_s, m_s, l_s, acc_s, sems = refs[16:]
    y, x, zl, core = pos_ref[0], pos_ref[1], pos_ref[2], pos_ref[3]
    y0 = lax.rem(y - zl + NY, NY)
    copies = []
    for j, step in enumerate((0, 1, 3, 2)):
        copies.append((q_in[j], q_s.at[lax.rem(x + step, NX)]))
    half = KT // 2
    for s in range(2):
        side = core if s == 0 else 1 - core
        at = pl.ds(pl.multiple_of(side * half, half), half)
        base = 5 * s
        for j, step in enumerate((0, 1, 3)):
            slot = lax.rem(y + step, NY) * 2
            for hi in range(2):
                copies.append((kv_in[base + j].at[pl.ds(hi * half, half)], kv_s.at[slot + hi, at]))
        slot = lax.rem(y + 2, NY) * 2
        for hi in range(2):
            copies.append((kv_in[base + 3 + hi], kv_s.at[slot + hi, at]))
    started = []
    for n, (src, dst) in enumerate(copies):
        c = pltpu.make_async_copy(src, dst, sems.at[n])
        c.start()
        started.append(c)
    for c in started:
        c.wait()

    def limit_of(p):
        out = ends_ref[3]
        for j in (2, 1, 0):
            out = jnp.where(p < ends_ref[j], ends_ref[j], out)
        return out

    def tile(t, carry):
        quarter_z = lax.div(t, 2)
        pair = lax.rem(t, 2)
        quarter = lax.rem(y0 + quarter_z, NY)
        first = quarter * 4096 + pair * 2048 + quarter_z * 128 + core * TOK
        low, high = limit_of(first), limit_of(first + 1599)
        full, seen = jnp.int32(0), jnp.int32(0)
        for c in range(8):
            start = (c // 2) * 4096 + (c % 2) * 512 + x * 1024
            full += jnp.where(start + 512 <= low, 1, 0)
            seen += jnp.where(start < high, 1, 0)
        for a in range(2):
            for b in range(2):
                qt_s[pl.ds((a * 2 + b) * TOK, TOK), :] = q_s[
                    2 * pair + a, pl.ds(pl.multiple_of((b * 4 + quarter_z) * TOK, TOK), TOK), :
                ]
        m_s[...] = jnp.full_like(m_s, NEG)
        l_s[...] = jnp.zeros_like(l_s)
        acc_s[...] = jnp.zeros_like(acc_s)

        def chunk(c, masked):
            if masked:
                row = lax.broadcasted_iota(jnp.int32, (QT, HD), 0)
                qpos = first + (row // 128) * 1024 + ((row // TOK) % 2) * 512 + row % TOK
                lim = limit_of(qpos)[:, :1]
                col = lax.broadcasted_iota(jnp.int32, (1, KT), 1)
                start = lax.div(c, 2) * 4096 + lax.rem(c, 2) * 512 + x * 1024
                kpos = start + ((col % 256) // TOK) * 128 + (col // 256) * TOK + col % TOK
                visible = kpos < lim
            for h in range(PER):
                q = qt_s[:, h * HD : (h + 1) * HD]
                k = kv_s[c, :, h * HD : (h + 1) * HD]
                v = kv_s[c, :, W + h * HD : W + (h + 1) * HD]
                s = lax.dot_general(q, k, (((1,), (1,)), ((), ())), preferred_element_type=jnp.float32)
                if masked:
                    s = jnp.where(visible, s, NEG)
                old = m_s[h]
                new = jnp.maximum(old, jnp.max(s, axis=1, keepdims=True))
                fade = jnp.exp2((old - new) * SCALE2)
                p = jnp.exp2((s - jnp.concatenate([new] * (KT // HD), axis=1)) * SCALE2)
                part = p[:, :HD]
                for g in range(1, KT // HD):
                    part = part + p[:, g * HD : (g + 1) * HD]
                l_s[h] = l_s[h] * fade + part
                acc_s[h] = acc_s[h] * fade + jnp.dot(
                    p.astype(jnp.bfloat16), v, preferred_element_type=jnp.float32
                )
                m_s[h] = new

        def full_chunk(c, carry):
            chunk(c, False)
            return carry

        def masked_chunk(c, carry):
            chunk(c, True)
            return carry

        lax.fori_loop(0, full, full_chunk, 0)
        lax.fori_loop(full, seen, masked_chunk, 0)
        lane = lax.broadcasted_iota(jnp.int32, (QT, HD), 1)
        lse = jnp.zeros((QT, HD), jnp.float32)
        for h in range(PER):
            total = jnp.sum(l_s[h], axis=1, keepdims=True)
            total = jnp.where(total == 0.0, 1.0, total)
            out = (acc_s[h] / total).astype(jnp.bfloat16)
            for a in range(2):
                for b in range(2):
                    o_ref[2 * pair + a, b * 4 + quarter_z, :, h * HD : (h + 1) * HD] = out[
                        (a * 2 + b) * TOK : (a * 2 + b + 1) * TOK
                    ]
            lse = jnp.where(lane == h, m_s[h] * SCALE2 + jnp.log2(total), lse)
        for a in range(2):
            for b in range(2):
                lse_ref[2 * pair + a, b * 4 + quarter_z] = lse[(a * 2 + b) * TOK : (a * 2 + b + 1) * TOK]
        return carry

    lax.fori_loop(0, 8, tile, 0)


def attention(ends, place, qs, kvs):
    n_copies = 4 + 16
    hbm = pl.BlockSpec(memory_space=pl.ANY)
    smem = pl.BlockSpec(memory_space=pltpu.SMEM)
    vmem = pl.BlockSpec(memory_space=pltpu.VMEM)
    return pl.pallas_call(
        attention_kernel,
        out_shape=(
            jax.ShapeDtypeStruct((NX, NZ, TOK, W), jnp.bfloat16),
            jax.ShapeDtypeStruct((NX, NZ, TOK, HD), jnp.float32),
        ),
        in_specs=[smem, smem] + [hbm] * 14,
        out_specs=(vmem, vmem),
        scratch_shapes=[
            pltpu.VMEM((NX, NZ * TOK, W), jnp.bfloat16),
            pltpu.VMEM((8, KT, 2 * W), jnp.bfloat16),
            pltpu.VMEM((QT, W), jnp.bfloat16),
            pltpu.VMEM((PER, QT, HD), jnp.float32),
            pltpu.VMEM((PER, QT, HD), jnp.float32),
            pltpu.VMEM((PER, QT, HD), jnp.float32),
            pltpu.SemaphoreType.DMA((n_copies,)),
        ],
        compiler_params=pltpu.CompilerParams(vmem_limit_bytes=48 * 1024 * 1024),
        cost_estimate=pl.CostEstimate(
            flops=12_900_000_000, bytes_accessed=10_000_000, transcendentals=25_000_000
        ),
        name="attention",
    )(ends, place, *qs, *kvs)


def ring(a, axis, step):
    return lax.ppermute(a, axis, [((i + step) % 4, i) for i in range(4)])


def swap(a):
    return lax.ppermute(a, "core", [(0, 1), (1, 0)])


SKEW_Q = [[((y0 + z) % NY) * NZ + z for z in range(NZ)] for y0 in range(NY)]
SKEW_O = [
    [(((y0 + z) % NY) * NX + x) * NZ + z for x in range(NX) for z in range(NZ)] for y0 in range(NY)
]


def local(queries, keys, values, residual, out_weight, gate_table, span_lengths, noise_levels):
    def by_group(a):
        return a.reshape(TOK, NZ, W).transpose(1, 0, 2)

    weight = lax.all_gather(out_weight, ("zl", "core"), axis=0, tiled=True)
    kv = jnp.concatenate([by_group(keys), by_group(values)], axis=2)
    kv = lax.all_to_all(kv, ("zh", "zl"), 0, 0, tiled=True).reshape(NZ * TOK, 2 * W)
    q = lax.all_to_all(
        by_group(queries), ("y", "zh", "zl"), 0, 0, tiled=True, axis_index_groups=SKEW_Q
    ).reshape(NZ * TOK, W)
    kv_p, kv_m = ring(kv, "y", 1), ring(kv, "y", 3)
    half = NZ * TOK // 2
    kv_2a = ring(kv_p[:half], "y", 1)
    kv_2b = ring(kv_m[half:], "y", 3)
    mine = [kv, kv_p, kv_m, kv_2a, kv_2b]
    other = [swap(a) for a in mine]
    q_p, q_m = ring(q, "x", 1), ring(q, "x", 3)
    q_2 = ring(q_p, "x", 1)
    ends = jnp.cumsum(span_lengths)
    y, x, zl, core = (lax.axis_index(n) for n in ("y", "x", "zl", "core"))
    z = lax.axis_index(("zh", "zl"))
    place = jnp.stack([y, x, zl, core]).astype(jnp.int32)
    out, lse = attention(ends, place, [q, q_p, q_m, q_2], mine + other)
    stat = lse[..., :PER]
    s1 = lax.reduce_precision(stat, 8, 7)
    r1 = stat - s1
    s2 = lax.reduce_precision(r1, 8, 7)
    s3 = r1 - s2
    stats = jnp.stack([s1, s2, s3], axis=2).astype(jnp.bfloat16)
    stats = stats.transpose(0, 1, 2, 4, 3).reshape(NX, NZ, 3 * PER * TOK)
    stats = jnp.pad(stats, ((0, 0), (0, 0), (0, 8 * W - 3 * PER * TOK))).reshape(NX, NZ, 8, W)
    sent = jnp.concatenate([out, stats], axis=2).reshape(NX * NZ, ROWS, W)
    got = lax.all_to_all(
        sent, ("y", "x", "zh", "zl"), 0, 0, tiled=True, axis_index_groups=SKEW_O
    ).reshape(NX, NZ, ROWS, W)
    part = got[:, :, :TOK].reshape(NX, NZ, TOK, PER, HD).astype(jnp.float32)
    stat = got[:, :, TOK:].reshape(NX, NZ, 8 * W)[:, :, : 3 * PER * TOK]
    stat = jnp.sum(stat.reshape(NX, NZ, 3, PER, TOK).astype(jnp.float32), axis=2)
    share = jnp.exp2(stat - jnp.max(stat, axis=0, keepdims=True))
    share = share / jnp.sum(share, axis=0, keepdims=True)
    share = share.transpose(0, 1, 3, 2)[..., None]
    attn = jnp.sum(part * share, axis=0).astype(jnp.bfloat16)
    attn = attn.transpose(1, 0, 2, 3).reshape(TOK, NZ * W)
    proj = jnp.dot(attn, weight, preferred_element_type=jnp.float32)
    first = (((y * NX + x) * NZ + z) * NC + core) * TOK
    tok = first + jnp.arange(TOK, dtype=jnp.int32)
    tok_span = jnp.sum((tok[:, None] >= ends[None, :]).astype(jnp.int32), axis=1)
    span_ids = jnp.arange(span_lengths.shape[0], dtype=jnp.int32)
    level = jnp.sum(jnp.where(tok_span[:, None] == span_ids[None, :], noise_levels[None, :], 0), axis=1)
    level_ids = jnp.arange(gate_table.shape[0], dtype=jnp.int32)
    one_hot = (level[:, None] == level_ids[None, :]).astype(jnp.float32)
    gate = jnp.dot(one_hot, gate_table, precision=lax.Precision.HIGHEST)
    return (residual.astype(jnp.float32) + gate * proj).astype(jnp.bfloat16)


def solution(mesh):
    fine = Mesh(mesh.devices.reshape(NY, NX, 2, 4, NC), ("y", "x", "zh", "zl", "core"))
    rows = P(("y", "x", "zh", "zl", "core"), None)
    return jax.shard_map(
        local,
        mesh=fine,
        in_specs=(rows, rows, rows, rows, P(("zl", "core"), None), P(), P(), P()),
        out_specs=rows,
        check_vma=False,
    )
```

time: 885 us -> 280 us (0.32)
  waiting for transfers between devices: 370 us -> 139 us
  matrix products: 211 us -> 11.9 us
  local copies, waits for them, and re-layouts: 126 us -> 17.3 us
  other arithmetic: 101 us -> 8.81 us
  Pallas kernels: 0 us -> 59.3 us
  blocking collectives: 34 us -> 0 us
  starting transfers between devices: 3.54 us -> 29.5 us
  loops' own time: 21.7 us -> 0 us
    all_gather x2 -> x1, waiting for transfers between devices: 318 us -> 12.1 us  [local(): weight = lax.all_gather(out_weight, ('zl', 'core'), axis=0, tiled=True)]
    dot_general x65 -> x1, matrix products: 209 us -> 10.5 us  [local(): proj = jnp.dot(attn, weight, preferred_element_type=jnp.float32)]
    all_to_all x1 -> x3, waiting for transfers between devices: 12.1 us -> 106 us  [the longest x1 61.4 us: local(): lax.all_to_all(sent, ('y', 'x', 'zh', 'zl'), 0, 0, tiled=True, axis_index...]
    reduce_sum x66 -> x4, other arithmetic: 91.2 us -> 2.94 us  [the longest x1 2.75 us: local(): attn = jnp.sum(part * share, axis=0).astype(jnp.bfloat16)]
    reshape x3 -> x4, local copies, waits for them, and re-layouts: 64.4 us -> 1.34 us  [the longest x1 0.79 us: by_group(): return a.reshape(TOK, NZ, W).transpose(1, 0, 2)]
    pallas_call x0 -> x1, Pallas kernels: none -> 59.3 us  [attention(): pl.pallas_call(attention_kernel, out_shape=(jax.ShapeDtypeStruct((NX, NZ,...]
    reduce_scatter x1 -> x0, waiting for transfers between devices: 40.2 us -> none  [local(): lax.psum_scatter(jnp.dot(attn, out_weight, preferred_element_type=jnp.flo...]
    all_to_all x2 -> x0, blocking collectives: 34 us -> none  [the longest x1 18.4 us: local(): lax.all_to_all(keys, 'head', split_axis=1, concat_axis=0, tiled=True)]
  transfers between devices with their start and end apart: 4 -> 16, of which waited for: 4 -> 9; matrix products, arithmetic and copies ran while one was open for 5% -> 8% of each run, Pallas kernels for 0% -> 21%
where the time goes in v1:
time: 280 us
  waiting for transfers between devices  139 us (50%)
  Pallas kernels  59.3 us (21%)
  starting transfers between devices  29.5 us (11%)
  local copies, waits for them, and re-layouts  17.3 us (6%)
  between operations  13.6 us (5%)
  matrix products  11.9 us (4%)
  other arithmetic  8.81 us (3%)
    all_to_all x1, waiting for transfers between devices, local(): lax.all_to_all(sent, ('y', 'x', 'zh', 'zl'), 0, 0, tiled=True, axis_index...  61.4 us
    pallas_call x1, Pallas kernels, attention(): pl.pallas_call(attention_kernel, out_shape=(jax.ShapeDtypeStruct((NX, NZ,...  59.3 us
    all_to_all x1, waiting for transfers between devices, local(): lax.all_to_all(kv, ('zh', 'zl'), 0, 0, tiled=True).reshape(NZ * TOK, 2 * W)  28.8 us
    ppermute x7, waiting for transfers between devices, ring(): return lax.ppermute(a, axis, [((i + step) % 4, i) for i in range(4)])  18.6 us
    all_to_all x1, waiting for transfers between devices, local(): lax.all_to_all(by_group(queries), ('y', 'zh', 'zl'), 0, 0, tiled=True, ax...  15.7 us
    all_gather x1, waiting for transfers between devices, local(): weight = lax.all_gather(out_weight, ('zl', 'core'), axis=0, tiled=True)  12.1 us
    dot_general x1, matrix products, local(): proj = jnp.dot(attn, weight, preferred_element_type=jnp.float32)  10.5 us
    all_to_all x1, starting transfers between devices, local(): lax.all_to_all(kv, ('zh', 'zl'), 0, 0, tiled=True).reshape(NZ * TOK, 2 * W)  8.6 us
  transfers between devices with their start and end apart: 16, of which 9 were waited for; matrix products, arithmetic and copies ran while one was open for 8% of the time, Pallas kernels for 21%

profile of v1, /device:TPU:2, one launch (start us, length us, event | category | flops | bytes accessed | tf_op | source)
XLA Modules:
  0.0 279.6 jit_solution(9178125219389376072)
XLA Ops:
  6.5 0.7 all-gather.2.cloned.1.call-update
  7.3 0.3 copy-done.9
  7.6 0.1 copy-done.8
  7.7 0.1 bitcast_bitcast_fusion
  7.8 1.0 pad_maximum_fusion.1
  8.8 8.6 %all-to-all-start.1 = ((bf16[8,64,768]{2,1,0:T(8,128)(2,1)}), bf16[8,64,768]{2,1,0:T(8,128)(2,1)S(1)}, u32[]{:S(2)}, u32[]{:S(2)}) async-start(bf16[8,64,768]{2,1,0:T(8,128)(2,1)} %pad_maximum_fusion.1), calls=%async_computation.1 | async-start | bytes 1572864 | tf_op jit(solution)/shard_map/all_to_all | solution.py:185
  17.4 0.8 copy.42
  18.2 28.8 %all-to-all-done.1 = bf16[8,64,768]{2,1,0:T(8,128)(2,1)S(1)} async-done(((bf16[8,64,768]{2,1,0:T(8,128)(2,1)}), bf16[8,64,768]{2,1,0:T(8,128)(2,1)S(1)}, u32[]{:S(2)}, u32[]{:S(2)}) %all-to-all-start.1) | async-done | bytes 786464 | tf_op jit(solution)/shard_map/all_to_all | solution.py:185
  47.0 4.6 %all-to-all-start = ((bf16[8,64,384]{2,1,0:T(8,128)(2,1)}), bf16[8,64,384]{2,1,0:T(8,128)(2,1)S(1)}, u32[]{:S(2)}, u32[]{:S(2)}) async-start(bf16[8,64,384]{2,1,0:T(8,128)(2,1)} %bitcast.53), calls=%async_computation | async-start | bytes 786432 | tf_op jit(solution)/shard_map/all_to_all | solution.py:186
  51.6 2.2 collective-permute-start.3
  53.8 15.7 %all-to-all-done = bf16[8,64,384]{2,1,0:T(8,128)(2,1)S(1)} async-done(((bf16[8,64,384]{2,1,0:T(8,128)(2,1)}), bf16[8,64,384]{2,1,0:T(8,128)(2,1)S(1)}, u32[]{:S(2)}, u32[]{:S(2)}) %all-to-all-start) | async-done | bytes 393248 | tf_op jit(solution)/shard_map/all_to_all | solution.py:186
  69.5 0.5 collective-permute-start
  70.0 1.5 collective-permute-start.1
  71.5 7.8 %collective-permute-done.refs_1_ = bf16[512,384]{1,0:T(8,128)(2,1)S(1)} collective-permute-done((bf16[512,384]{1,0:T(8,128)(2,1)S(1)}, bf16[512,384]{1,0:T(8,128)(2,1)S(1)}, u32[]{:S(2)}, u32[]{:S(2)}) %collective-permute-start) | collective-permute-done | bytes 393248 | tf_op jit(solution)/shard_map/ppermute | solution.py:166
  79.4 0.8 collective-permute-start.2
  80.2 3.4 %collective-permute-start.5 = (bf16[256,768]{1,0:T(8,128)(2,1)S(1)}, bf16[256,768]{1,0:T(8,128)(2,1)}, u32[]{:S(2)}, u32[]{:S(2)}) collective-permute-start(bf16[256,768]{1,0:T(8,128)(2,1)S(1)} %slice.24), channel_id=1, source_target_pairs={{64,0},{128,64},{192,128},{0,192},{65,1},{129,65},{193,129},{1,193... | collective-permute-start | bytes 1179656 | tf_op jit(solution)/shard_map/ppermute | solution.py:166
  83.8 0.7 copy-done.1
  84.5 0.2 collective-permute-start.8
  84.7 3.7 %collective-permute-done.2.refs_3_ = bf16[512,384]{1,0:T(8,128)(2,1)S(1)} collective-permute-done((bf16[512,384]{1,0:T(8,128)(2,1)S(1)}, bf16[512,384]{1,0:T(8,128)(2,1)S(1)}, u32[]{:S(2)}, u32[]{:S(2)}) %collective-permute-start.2) | collective-permute-done | bytes 393248 | tf_op jit(solution)/shard_map/ppermute | solution.py:166
  88.4 0.8 copy-done.3
  89.2 3.5 %collective-permute-done.5.refs_7_ = bf16[256,768]{1,0:T(8,128)(2,1)} collective-permute-done((bf16[256,768]{1,0:T(8,128)(2,1)S(1)}, bf16[256,768]{1,0:T(8,128)(2,1)}, u32[]{:S(2)}, u32[]{:S(2)}) %collective-permute-start.5) | collective-permute-done | bytes 393248 | tf_op jit(solution)/shard_map/ppermute | solution.py:166
  92.7 3.6 %collective-permute-done.6.refs_8_ = bf16[256,768]{1,0:T(8,128)(2,1)} collective-permute-done((bf16[256,768]{1,0:T(8,128)(2,1)S(1)}, bf16[256,768]{1,0:T(8,128)(2,1)}, u32[]{:S(2)}, u32[]{:S(2)}) %collective-permute-start.6) | collective-permute-done | bytes 393248 | tf_op jit(solution)/shard_map/ppermute | solution.py:166
  96.3 0.2 reduce-window.8
  96.5 1.8 collective-permute-done.11.refs_13_
  98.4 1.0 copy-done.2
  99.4 1.0 copy-done.4
  100.4 59.3 %attention.1 = (bf16[4,8,64,384]{3,2,1,0:T(8,128)(2,1)}, f32[4,8,64,128]{3,2,1,0:T(8,128)}) custom-call(s32[4]{0:T(128)S(1)} %bitcast.61, s32[4]{0:T(128)S(1)} %pad_add_fusion.pos_ref, bf16[512,384]{1,0:T(8,128)(2,1)S(1)} %bitcast.60, bf16[512,384]{1,0:T(8,128)(2,1)S(1)} %collective-permute-done.refs_1_, bf16[512,384]{1,0:T(8,128)(2,1)S(1)} %copy-done.2, ...), custom_call_target="tpu_custom_call" | custom-call | flops 12899999744 | bytes 10000000 | tf_op jit(solution)/shard_map/attention/pallas_call | solution.py:140
  159.6 1.7 fusion.4
  161.3 0.3 copy.29
  161.6 0.3 copy.30
  161.8 0.3 copy.31
  162.2 0.1 reshape.79
  162.4 2.8 %pad_maximum_fusion = bf16[32,72,384]{2,1,0:T(8,128)(2,1)} fusion(bf16[32,8,384]{2,1,0:T(8,128)(2,1)S(1)} %bitcast.67, bf16[32,64,384]{2,1,0:T(8,128)(2,1)} %bitcast.66), kind=kLoop, calls=%fused_computation.4 | loop fusion | flops 3538944 | bytes 3538944 | tf_op jit(solution)/shard_map/concatenate | solution.py:210
  165.2 7.6 %all-to-all-start.2 = ((bf16[32,72,384]{2,1,0:T(8,128)(2,1)}), bf16[32,72,384]{2,1,0:T(8,128)(2,1)S(1)}, u32[]{:S(2)}, u32[]{:S(2)}) async-start(bf16[32,72,384]{2,1,0:T(8,128)(2,1)} %pad_maximum_fusion), calls=%async_computation.2 | async-start | bytes 3538944 | tf_op jit(solution)/shard_map/all_to_all | solution.py:211
  173.0 1.4 fusion.9
  174.4 61.4 %all-to-all-done.2 = bf16[32,72,384]{2,1,0:T(8,128)(2,1)S(1)} async-done(((bf16[32,72,384]{2,1,0:T(8,128)(2,1)}), bf16[32,72,384]{2,1,0:T(8,128)(2,1)S(1)}, u32[]{:S(2)}, u32[]{:S(2)}) %all-to-all-start.2) | async-done | bytes 1769504 | tf_op jit(solution)/shard_map/all_to_all | solution.py:211
  235.8 0.1 reshape.81
  235.9 0.1 reshape.83
  236.2 0.4 copy.33
  236.6 0.3 copy-done.5
  237.0 3.9 %mul.34 = f32[4,8,64,3,128]{4,3,2,1,0:T(4,128)} broadcast(f32[4,8,64,3]{3,2,1,0:T(8,128)S(1)} %copy.33), dimensions={0,1,2,3} | broadcast | bytes 3170304 | tf_op jit(solution)/shard_map/mul | solution.py:220
  240.8 4.5 %mul.35 = f32[4,8,64,384]{3,2,1,0:T(8,128)S(1)} reshape(f32[4,8,64,3,128]{4,3,2,1,0:T(4,128)} %mul.34) | data formatting | bytes 6291456 | tf_op jit(solution)/shard_map/mul | solution.py:220
  245.4 2.7 multiply_reduce_fusion
  248.1 1.5 convert_element_type.39
  249.6 0.2 copy.34
  249.8 0.3 reshape.82
  250.2 12.1 %all-gather.2.cloned.1.call-done = bf16[3072,3072]{1,0:T(8,128)(2,1)} async-done(((bf16[384,3072]{1,0:T(8,128)(2,1)}), bf16[3072,3072]{1,0:T(8,128)(2,1)}) %all-gather.2.cloned.1.call-update) | async-done | bytes 18874384 | tf_op jit(solution)/shard_map/all_gather | solution.py:183
  262.2 10.5 %fusion.1 = bf16[64,3072]{1,0:T(8,128)(2,1)} fusion(f32[64,3072]{1,0:T(8,128)S(1)} %copy-done.6, bf16[64,3072]{1,0:T(8,128)(2,1)S(1)} %reshape.82, bf16[3072,3072]{1,0:T(8,128)(2,1)} %all-gather.2.cloned.1.call-done, bf16[64,3072]{1,0:T(8,128)(2,1)S(1)} %copy-done.10), kind=kOutput, calls=%fused_computation.2 | convolution fusion | flops 1208745984 | bytes 20840448 | tf_op jit(solution)/shard_map/dot_general | solution.py:222
  (49 shorter events, 0.8 us)
Async XLA Ops:
  6.5 166.5 %copy-start = (f32[8,3072]{1,0:T(8,128)S(1)}, f32[8,3072]{1,0:T(8,128)}, u32[]{:S(2)}) copy-start(f32[8,3072]{1,0:T(8,128)} %param.13) | copy-start | bytes 294916
  6.5 1.0 copy-start.9
  6.5 1.1 copy-start.8
  6.5 255.7 %all-gather.2.cloned.1.call-start = ((), (), s32[]{:S(2)}) async-start(), calls=%async_computation.3 | async-start | bytes 21233664 | tf_op jit(solution)/shard_map/all_gather | solution.py:183
  7.7 9.7 %copy-start.7 = (bf16[64,3072]{1,0:T(8,128)(2,1)S(1)}, bf16[64,3072]{1,0:T(8,128)(2,1)}, u32[]{:S(2)}) copy-start(bf16[64,3072]{1,0:T(8,128)(2,1)} %param.8) | copy-start | bytes 1179652
  8.8 87.5 %copy-start.11 = (s32[4]{0:T(128)S(1)}, s32[4]{0:T(128)}, u32[]{:S(2)}) copy-start(s32[4]{0:T(128)} %param.14) | copy-start | bytes 52
  8.8 38.2 %all-to-all-start.1 = ((bf16[8,64,768]{2,1,0:T(8,128)(2,1)}), bf16[8,64,768]{2,1,0:T(8,128)(2,1)S(1)}, u32[]{:S(2)}, u32[]{:S(2)}) async-start(bf16[8,64,768]{2,1,0:T(8,128)(2,1)} %pad_maximum_fusion.1), calls=%async_computation.1 | async-start | bytes 1572864 | tf_op jit(solution)/shard_map/all_to_all | solution.py:185
  47.0 22.5 %all-to-all-start = ((bf16[8,64,384]{2,1,0:T(8,128)(2,1)}), bf16[8,64,384]{2,1,0:T(8,128)(2,1)S(1)}, u32[]{:S(2)}, u32[]{:S(2)}) async-start(bf16[8,64,384]{2,1,0:T(8,128)(2,1)} %bitcast.53), calls=%async_computation | async-start | bytes 786432 | tf_op jit(solution)/shard_map/all_to_all | solution.py:186
  51.6 28.6 %collective-permute-start.3 = (bf16[512,768]{1,0:T(8,128)(2,1)S(1)}, bf16[512,768]{1,0:T(8,128)(2,1)S(1)}, u32[]{:S(2)}, u32[]{:S(2)}) collective-permute-start(bf16[512,768]{1,0:T(8,128)(2,1)S(1)} %bitcast.54), channel_id=1, source_target_pairs={{64,0},{128,64},{192,128},{0,192},{65,1},{129,65},{193,129},{1,193... | collective-permute-start | bytes 2359304 | tf_op jit(solution)/shard_map/ppermute | solution.py:166
  53.8 29.8 %collective-permute-start.4 = (bf16[512,768]{1,0:T(8,128)(2,1)S(1)}, bf16[512,768]{1,0:T(8,128)(2,1)S(1)}, u32[]{:S(2)}, u32[]{:S(2)}) collective-permute-start(bf16[512,768]{1,0:T(8,128)(2,1)S(1)} %bitcast.55), channel_id=1, source_target_pairs={{192,0},{0,64},{64,128},{128,192},{193,1},{1,65},{65,129},{129,193... | collective-permute-start | bytes 2359304 | tf_op jit(solution)/shard_map/ppermute | solution.py:166
  69.5 9.9 %collective-permute-start = (bf16[512,384]{1,0:T(8,128)(2,1)S(1)}, bf16[512,384]{1,0:T(8,128)(2,1)S(1)}, u32[]{:S(2)}, u32[]{:S(2)}) collective-permute-start(bf16[512,384]{1,0:T(8,128)(2,1)S(1)} %bitcast.58), channel_id=1, source_target_pairs={{16,0},{32,16},{48,32},{0,48},{17,1},{33,17},{49,33},{1,49},{18,2}... | collective-permute-start | bytes 1179656 | tf_op jit(solution)/shard_map/ppermute | solution.py:166
  70.0 13.7 %collective-permute-start.1 = (bf16[512,384]{1,0:T(8,128)(2,1)S(1)}, bf16[512,384]{1,0:T(8,128)(2,1)S(1)}, u32[]{:S(2)}, u32[]{:S(2)}) collective-permute-start(bf16[512,384]{1,0:T(8,128)(2,1)S(1)} %bitcast.59), channel_id=1, source_target_pairs={{48,0},{0,16},{16,32},{32,48},{49,1},{1,17},{17,33},{33,49},{50,2}... | collective-permute-start | bytes 1179656 | tf_op jit(solution)/shard_map/ppermute | solution.py:166
  79.4 9.1 %collective-permute-start.2 = (bf16[512,384]{1,0:T(8,128)(2,1)S(1)}, bf16[512,384]{1,0:T(8,128)(2,1)S(1)}, u32[]{:S(2)}, u32[]{:S(2)}) collective-permute-start(bf16[512,384]{1,0:T(8,128)(2,1)S(1)} %collective-permute-done.refs_1_), channel_id=1, source_target_pairs={{16,0},{32,16},{48,32},{0,48},{17,1},{33,17},{49,33},{1,49},{18,2}... | collective-permute-start | bytes 1179656 | tf_op jit(solution)/shard_map/ppermute | solution.py:166
  80.2 16.4 %collective-permute-start.7 = (bf16[512,768]{1,0:T(8,128)(2,1)S(1)}, bf16[512,768]{1,0:T(8,128)(2,1)}, u32[]{:S(2)}, u32[]{:S(2)}) collective-permute-start(bf16[512,768]{1,0:T(8,128)(2,1)S(1)} %bitcast.56), channel_id=1, source_target_pairs={{0,1},{1,0},{2,3},{3,2},{4,5},{5,4},{6,7},{7,6},{8,9},{9,8},{10,11... | collective-permute-start | bytes 2359304 | tf_op jit(solution)/shard_map/ppermute | solution.py:170
  80.2 12.4 %collective-permute-start.5 = (bf16[256,768]{1,0:T(8,128)(2,1)S(1)}, bf16[256,768]{1,0:T(8,128)(2,1)}, u32[]{:S(2)}, u32[]{:S(2)}) collective-permute-start(bf16[256,768]{1,0:T(8,128)(2,1)S(1)} %slice.24), channel_id=1, source_target_pairs={{64,0},{128,64},{192,128},{0,192},{65,1},{129,65},{193,129},{1,193... | collective-permute-start | bytes 1179656 | tf_op jit(solution)/shard_map/ppermute | solution.py:166
  83.6 12.6 %collective-permute-start.6 = (bf16[256,768]{1,0:T(8,128)(2,1)S(1)}, bf16[256,768]{1,0:T(8,128)(2,1)}, u32[]{:S(2)}, u32[]{:S(2)}) collective-permute-start(bf16[256,768]{1,0:T(8,128)(2,1)S(1)} %slice.25), channel_id=1, source_target_pairs={{192,0},{0,64},{64,128},{128,192},{193,1},{1,65},{65,129},{129,193... | collective-permute-start | bytes 1179656 | tf_op jit(solution)/shard_map/ppermute | solution.py:166
  83.7 0.7 copy-start.1
  84.5 13.9 %collective-permute-start.8 = (bf16[512,768]{1,0:T(8,128)(2,1)S(1)}, bf16[512,768]{1,0:T(8,128)(2,1)}, u32[]{:S(2)}, u32[]{:S(2)}) collective-permute-start(bf16[512,768]{1,0:T(8,128)(2,1)S(1)} %collective-permute-done.3.refs_5_), channel_id=1, source_target_pairs={{0,1},{1,0},{2,3},{3,2},{4,5},{5,4},{6,7},{7,6},{8,9},{9,8},{10,11... | collective-permute-start | bytes 2359304 | tf_op jit(solution)/shard_map/ppermute | solution.py:170
  88.4 0.8 copy-start.3
  89.2 9.2 %collective-permute-start.9 = (bf16[512,768]{1,0:T(8,128)(2,1)S(1)}, bf16[512,768]{1,0:T(8,128)(2,1)}, u32[]{:S(2)}, u32[]{:S(2)}) collective-permute-start(bf16[512,768]{1,0:T(8,128)(2,1)S(1)} %collective-permute-done.4.refs_6_), channel_id=1, source_target_pairs={{0,1},{1,0},{2,3},{3,2},{4,5},{5,4},{6,7},{7,6},{8,9},{9,8},{10,11... | collective-permute-start | bytes 2359304 | tf_op jit(solution)/shard_map/ppermute | solution.py:170
  92.6 3.9 %collective-permute-start.10 = (bf16[256,768]{1,0:T(8,128)(2,1)}, bf16[256,768]{1,0:T(8,128)(2,1)}, u32[]{:S(2)}, u32[]{:S(2)}) collective-permute-start(bf16[256,768]{1,0:T(8,128)(2,1)} %collective-permute-done.5.refs_7_), channel_id=1, source_target_pairs={{0,1},{1,0},{2,3},{3,2},{4,5},{5,4},{6,7},{7,6},{8,9},{9,8},{10,11... | collective-permute-start | bytes 1179656 | tf_op jit(solution)/shard_map/ppermute | solution.py:170
  96.3 2.1 collective-permute-start.11
  98.3 1.0 copy-start.2
  99.4 1.0 copy-start.4
  165.2 7.7 %copy-start.12 = (s32[4]{0:T(128)S(1)}, s32[4]{0:T(128)}, u32[]{:S(2)}) copy-start(s32[4]{0:T(128)} %param.15) | copy-start | bytes 52
  165.2 70.6 %all-to-all-start.2 = ((bf16[32,72,384]{2,1,0:T(8,128)(2,1)}), bf16[32,72,384]{2,1,0:T(8,128)(2,1)S(1)}, u32[]{:S(2)}, u32[]{:S(2)}) async-start(bf16[32,72,384]{2,1,0:T(8,128)(2,1)} %pad_maximum_fusion), calls=%async_computation.2 | async-start | bytes 3538944 | tf_op jit(solution)/shard_map/all_to_all | solution.py:211
  235.8 1.2 copy-start.5
  248.1 14.1 %copy-start.6 = (f32[64,3072]{1,0:T(8,128)S(1)}, f32[64,3072]{1,0:T(8,128)}, u32[]{:S(2)}) copy-start(f32[64,3072]{1,0:T(8,128)} %fusion.9) | copy-start | bytes 2359300
  248.1 14.1 %copy-start.10 = (bf16[64,3072]{1,0:T(8,128)(2,1)S(1)}, bf16[64,3072]{1,0:T(8,128)(2,1)}, u32[]{:S(2)}) copy-start(bf16[64,3072]{1,0:T(8,128)(2,1)} %param.11) | copy-start | bytes 1179652
Sparse Core Ops, SparseCore 0:
  9.2 253.0 all-gather.1

commit v2 on v1

v2 whole, which is shorter than its diff:
```python
import jax
import jax.numpy as jnp
from jax import lax
from jax.sharding import Mesh, PartitionSpec as P
from jax.experimental import pallas as pl
from jax.experimental.pallas import tpu as pltpu

HD = 128
PER = 3
W = PER * HD
TOK = 64
SCALE2 = HD ** (-0.5) * 1.4426950408889634
NEG = -1e30
NY, NX, NZ, NC = 4, 4, 8, 2
NXT = 2
QT = NXT * 2 * TOK
KT = 512
PAIR = 2
QROWS = NZ * TOK
SROWS = 32
ROWS = QROWS + SROWS
D = 3072


def attention_kernel(ends_ref, pos_ref, *refs):
    q_in = refs[0]
    kv_in = refs[1:11]
    o_ref = refs[11]
    q_s, kv_s, qt_s, m_s, l_s, acc_s, lse_s, sems = refs[12:]
    y, x, zl, core = pos_ref[0], pos_ref[1], pos_ref[2], pos_ref[3]
    y0 = lax.rem(y - zl + NY, NY)
    copies = [(q_in, q_s)]
    for s in range(2):
        side = core if s == 0 else 1 - core
        base = 5 * s
        for j, step in enumerate((0, 1, 3, 2)):
            for n in range(NZ):
                quarter = lax.rem(y0 + step + n, NY)
                at = (quarter * 2 + n // 4) * KT + side * (KT // 2) + (n % 4) * TOK
                dst = kv_s.at[pl.ds(pl.multiple_of(at, TOK), TOK)]
                if j < 3:
                    src = kv_in[base + j].at[pl.ds(n * TOK, TOK)]
                else:
                    src = kv_in[base + 3 + n // 4].at[pl.ds((n % 4) * TOK, TOK)]
                copies.append((src, dst))
    started = []
    for n, (src, dst) in enumerate(copies):
        c = pltpu.make_async_copy(src, dst, sems.at[n])
        c.start()
        started.append(c)
    for c in started:
        c.wait()

    def limit_of(p):
        out = ends_ref[3]
        for j in (2, 1, 0):
            out = jnp.where(p < ends_ref[j], ends_ref[j], out)
        return out

    def tile(t, carry):
        quarter_z = lax.div(t, NX // NXT)
        part_x = lax.rem(t, NX // NXT) * NXT
        quarter = lax.rem(y0 + quarter_z, NY)
        first = quarter * 4096 + part_x * 1024 + quarter_z * 128 + core * TOK
        low, high = limit_of(first), limit_of(first + (NXT - 1) * 1024 + 512 + TOK - 1)
        full, seen = jnp.int32(0), jnp.int32(0)
        for c in range(8):
            start = (c // 2) * 4096 + (c % 2) * 512 + x * 1024
            full += jnp.where(start + 512 <= low, 1, 0)
            seen += jnp.where(start < high, 1, 0)
        for a in range(NXT):
            for b in range(2):
                qt_s[pl.ds((a * 2 + b) * TOK, TOK), :] = q_s[
                    part_x + a, pl.ds(pl.multiple_of((b * 4 + quarter_z) * TOK, TOK), TOK), :
                ]
        m_s[...] = jnp.full_like(m_s, NEG)
        l_s[...] = jnp.zeros_like(l_s)
        acc_s[...] = jnp.zeros_like(acc_s)

        def chunk(c, size, masked):
            keys = size * KT
            rows = pl.ds(pl.multiple_of(c * KT, KT), keys)
            if masked:
                row = lax.broadcasted_iota(jnp.int32, (QT, HD), 0)
                qpos = first + (row // 128) * 1024 + ((row // TOK) % 2) * 512 + row % TOK
                lim = limit_of(qpos)[:, :1]
                col = lax.broadcasted_iota(jnp.int32, (1, KT), 1)
                start = lax.div(c, 2) * 4096 + lax.rem(c, 2) * 512 + x * 1024
                kpos = start + ((col % 256) // TOK) * 128 + (col // 256) * TOK + col % TOK
                visible = kpos < lim

            def score(h):
                q = qt_s[:, h * HD : (h + 1) * HD]
                k = kv_s[rows, h * HD : (h + 1) * HD]
                return lax.dot_general(q, k, (((1,), (1,)), ((), ())), preferred_element_type=jnp.float32)

            ahead = score(0)
            for h in range(PER):
                s = ahead
                if h + 1 < PER:
                    ahead = score(h + 1)
                v = kv_s[rows, W + h * HD : W + (h + 1) * HD]
                if masked:
                    s = jnp.where(visible, s, NEG)
                old = m_s[h]
                new = jnp.maximum(old, jnp.max(s, axis=1, keepdims=True))
                fade = jnp.exp2((old - new) * SCALE2)
                p = jnp.exp2((s - jnp.concatenate([new] * (keys // HD), axis=1)) * SCALE2)
                part = p[:, :HD]
                for g in range(1, keys // HD):
                    part = part + p[:, g * HD : (g + 1) * HD]
                l_s[h] = l_s[h] * fade + part
                acc_s[h] = acc_s[h] * fade + jnp.dot(
                    p.astype(jnp.bfloat16), v, preferred_element_type=jnp.float32
                )
                m_s[h] = new

        def full_chunk(c, carry):
            chunk(c * PAIR, PAIR, False)
            return carry

        def masked_chunk(c, carry):
            chunk(c, 1, True)
            return carry

        whole = lax.div(full, PAIR)
        lax.fori_loop(0, whole, full_chunk, 0)
        lax.fori_loop(whole * PAIR, seen, masked_chunk, 0)
        lane = lax.broadcasted_iota(jnp.int32, (QT, HD), 1)
        lse = jnp.zeros((QT, HD), jnp.float32)
        for h in range(PER):
            total = jnp.sum(l_s[h], axis=1, keepdims=True)
            total = jnp.where(total == 0.0, 1.0, total)
            out = (acc_s[h] / total).astype(jnp.bfloat16)
            for a in range(NXT):
                for b in range(2):
                    at = pl.ds(pl.multiple_of((b * 4 + quarter_z) * TOK, TOK), TOK)
                    o_ref[part_x + a, at, h * HD : (h + 1) * HD] = out[
                        (a * 2 + b) * TOK : (a * 2 + b + 1) * TOK
                    ]
            lse = jnp.where(lane == h, m_s[h] * SCALE2 + jnp.log2(total), lse)
        for a in range(NXT):
            for b in range(2):
                at = pl.ds(pl.multiple_of((b * 4 + quarter_z) * TOK, TOK), TOK)
                lse_s[part_x + a, at, :] = lse[(a * 2 + b) * TOK : (a * 2 + b + 1) * TOK]
        return carry

    lax.fori_loop(0, 4 * NX // NXT, tile, 0)
    for a in range(NX):
        stat = jnp.concatenate(
            [lse_s[a, g * HD : (g + 1) * HD, :].T[:8] for g in range(QROWS // HD)], axis=0
        )
        for n in range(3):
            part = stat.astype(jnp.bfloat16)
            o_ref[a, QROWS:, n * HD : (n + 1) * HD] = part
            stat = stat - part.astype(jnp.float32)


def attention(ends, place, q_all, kvs):
    n_copies = 1 + 64
    hbm = pl.BlockSpec(memory_space=pl.ANY)
    smem = pl.BlockSpec(memory_space=pltpu.SMEM)
    vmem = pl.BlockSpec(memory_space=pltpu.VMEM)
    return pl.pallas_call(
        attention_kernel,
        out_shape=jax.ShapeDtypeStruct((NX, ROWS, W), jnp.bfloat16),
        in_specs=[smem, smem] + [hbm] * 11,
        out_specs=vmem,
        scratch_shapes=[
            pltpu.VMEM((NX, QROWS, W), jnp.bfloat16),
            pltpu.VMEM((8 * KT, 2 * W), jnp.bfloat16),
            pltpu.VMEM((QT, W), jnp.bfloat16),
            pltpu.VMEM((PER, QT, HD), jnp.float32),
            pltpu.VMEM((PER, QT, HD), jnp.float32),
            pltpu.VMEM((PER, QT, HD), jnp.float32),
            pltpu.VMEM((NX, QROWS, HD), jnp.float32),
            pltpu.SemaphoreType.DMA((n_copies,)),
        ],
        compiler_params=pltpu.CompilerParams(vmem_limit_bytes=48 * 1024 * 1024),
        cost_estimate=pl.CostEstimate(
            flops=1_000_000, bytes_accessed=1_000_000, transcendentals=1_000
        ),
        name="attention",
    )(ends, place, q_all, *kvs)


def combine_kernel(got_ref, o_ref):
    logs = []
    for j in range(NX):
        parts = got_ref[j, QROWS:, :].astype(jnp.float32)
        logs.append(parts[:, :HD] + parts[:, HD : 2 * HD] + parts[:, 2 * HD :])
    peak = jnp.maximum(jnp.maximum(logs[0], logs[1]), jnp.maximum(logs[2], logs[3]))
    shares = [jnp.exp2(v - peak) for v in logs]
    total = shares[0] + shares[1] + shares[2] + shares[3]
    shares = [v / total for v in shares]
    for g in range(QROWS // HD):
        rows = [v[g * 8 : (g + 1) * 8] for v in shares]
        columns = jnp.concatenate(rows + [jnp.zeros((HD - 8 * NX, HD), jnp.float32)], axis=0).T
        at = slice(g * HD, (g + 1) * HD)
        for h in range(PER):
            out = jnp.zeros((HD, HD), jnp.float32)
            for j in range(NX):
                part = got_ref[j, at, h * HD : (h + 1) * HD].astype(jnp.float32)
                out = out + part * columns[:, j * 8 + h : j * 8 + h + 1]
            o_ref[at, h * HD : (h + 1) * HD] = out.astype(jnp.bfloat16)


def combine(got):
    vmem = pl.BlockSpec(memory_space=pltpu.VMEM)
    return pl.pallas_call(
        combine_kernel,
        out_shape=jax.ShapeDtypeStruct((QROWS, W), jnp.bfloat16),
        in_specs=[vmem],
        out_specs=vmem,
        compiler_params=pltpu.CompilerParams(vmem_limit_bytes=16 * 1024 * 1024),
        cost_estimate=pl.CostEstimate(flops=4_000_000, bytes_accessed=2_500_000, transcendentals=20_000),
        name="combine",
    )(got)


def project_kernel(pos_ref, keep_ref, got_ref, *refs):
    w_in = refs[:5]
    o_ref = refs[5]
    w_s, acc_s, sems = refs[6:]
    zl = pos_ref[2]
    started = []
    wide = D // 2
    for j in range(5):
        dst = w_s.at[j] if j < 3 else w_s.at[3, :, pl.ds((j - 3) * wide, wide)]
        c = pltpu.make_async_copy(w_in[j], dst, sems.at[j])
        c.start()
        started.append(c)
    acc_s[...] = jnp.zeros_like(acc_s)
    for j, step in enumerate((0, 1, 3, 2)):
        started[j].wait()
        if j == 3:
            started[4].wait()
        row = lax.rem(zl + step, 4)
        lhs = jnp.concatenate([keep_ref[row], got_ref[row]], axis=0)
        acc_s[...] += jnp.dot(lhs, w_s[j], preferred_element_type=jnp.float32)
    o_ref[0] = acc_s[:TOK].astype(jnp.bfloat16)
    o_ref[1] = acc_s[TOK:].astype(jnp.bfloat16)


def project(place, keep, got, weights):
    vmem = pl.BlockSpec(memory_space=pltpu.VMEM)
    return pl.pallas_call(
        project_kernel,
        out_shape=jax.ShapeDtypeStruct((2, TOK, D), jnp.bfloat16),
        in_specs=[pl.BlockSpec(memory_space=pltpu.SMEM), vmem, vmem]
        + [pl.BlockSpec(memory_space=pl.ANY)] * 5,
        out_specs=vmem,
        scratch_shapes=[
            pltpu.VMEM((4, W, D), jnp.bfloat16),
            pltpu.VMEM((2 * TOK, D), jnp.float32),
            pltpu.SemaphoreType.DMA((5,)),
        ],
        compiler_params=pltpu.CompilerParams(vmem_limit_bytes=28 * 1024 * 1024),
        cost_estimate=pl.CostEstimate(
            flops=2 * TOK * D * D, bytes_accessed=10_000_000, transcendentals=0
        ),
        name="project",
    )(place, keep, got, *weights)


def after(token, arrays):
    hbm = pl.BlockSpec(memory_space=pl.ANY)

    def kernel(*refs):
        pass

    return pl.pallas_call(
        kernel,
        out_shape=[jax.ShapeDtypeStruct(a.shape, a.dtype) for a in arrays],
        in_specs=[hbm] * (1 + len(arrays)),
        out_specs=[hbm] * len(arrays),
        input_output_aliases={n + 1: n for n in range(len(arrays))},
        name="after",
    )(token, *arrays)


def ring(a, axis, step):
    return lax.ppermute(a, axis, [((i + step) % 4, i) for i in range(4)])


def swap(a):
    return lax.ppermute(a, "core", [(0, 1), (1, 0)])


SKEW = [[((y0 + z) % NY) * NZ + z for z in range(NZ)] for y0 in range(NY)]


def skewed(a):
    return lax.all_to_all(a, ("y", "zh", "zl"), 0, 0, tiled=True, axis_index_groups=SKEW)


def ring_z(a, step):
    return lax.ppermute(a, ("zh", "zl"), [((i + step) % NZ, i) for i in range(NZ)])


def local(queries, keys, values, residual, out_weight, gate_table, span_lengths, noise_levels):
    def by_group(a):
        return a.reshape(TOK, NZ, W).transpose(1, 0, 2)

    qkv = jnp.concatenate([by_group(queries), by_group(keys), by_group(values)], axis=2)
    qkv = skewed(qkv).reshape(QROWS, 3 * W)
    q, kv = qkv[:, :W], qkv[:, W:]
    kv_p, kv_m = ring(kv, "y", 1), ring(kv, "y", 3)
    half = QROWS // 2
    kv_2a = ring(kv_p[:half], "y", 1)
    kv_2b = ring(kv_m[half:], "y", 3)
    mine = [kv, kv_p, kv_m, kv_2a, kv_2b]
    other = [swap(a) for a in mine]
    q_all = lax.all_to_all(jnp.broadcast_to(q[None], (NX, QROWS, W)), "x", 0, 0, tiled=True)
    arrived = q[0, 0] == q[0, 0]
    w_late = jnp.where(arrived, out_weight, jnp.zeros_like(out_weight))
    w_p, w_m = ring_z(w_late, 1), ring_z(w_late, 7)
    ends = jnp.cumsum(span_lengths)
    y, x, zl, core = (lax.axis_index(n) for n in ("y", "x", "zl", "core"))
    z = lax.axis_index(("zh", "zl"))
    place = jnp.stack([y, x, zl, core]).astype(jnp.int32)
    sent = attention(ends, place, q_all, mine + other)
    w_p, w_m = after(sent, [w_p, w_m])
    w_2a, w_2b = ring_z(w_p[:, : D // 2], 1), ring_z(w_m[:, D // 2 :], 7)
    attn = combine(lax.all_to_all(sent, "x", 0, 0, tiled=True))
    w_2a, w_2b = after(attn, [w_2a, w_2b])
    attn = skewed(attn.reshape(NZ, TOK, W)).reshape(NZ // NC, NC, TOK, W)
    low = core == 0
    keep = jnp.where(low, attn[:, 0], attn[:, 1])
    other_attn = swap(jnp.where(low, attn[:, 1], attn[:, 0]))
    terms = project(place, keep, other_attn, [w_late, w_p, w_m, w_2a, w_2b])
    proj = terms[0].astype(jnp.float32) + swap(terms[1]).astype(jnp.float32)
    first = (((y * NX + x) * NZ + z) * NC + core) * TOK
    tok = first + jnp.arange(TOK, dtype=jnp.int32)
    tok_span = jnp.sum((tok[:, None] >= ends[None, :]).astype(jnp.int32), axis=1)
    span_ids = jnp.arange(span_lengths.shape[0], dtype=jnp.int32)
    level = jnp.sum(jnp.where(tok_span[:, None] == span_ids[None, :], noise_levels[None, :], 0), axis=1)
    level_ids = jnp.arange(gate_table.shape[0], dtype=jnp.int32)
    one_hot = (level[:, None] == level_ids[None, :]).astype(jnp.float32)
    gate = jnp.dot(one_hot, gate_table, precision=lax.Precision.HIGHEST)
    return (residual.astype(jnp.float32) + gate * proj).astype(jnp.bfloat16)


def solution(mesh):
    fine = Mesh(mesh.devices.reshape(NY, NX, 2, 4, NC), ("y", "x", "zh", "zl", "core"))
    rows = P(("y", "x", "zh", "zl", "core"), None)
    return jax.shard_map(
        local,
        mesh=fine,
        in_specs=(rows, rows, rows, rows, P(("zl", "core"), None), P(), P(), P()),
        out_specs=rows,
        check_vma=False,
    )
```

time: 280 us -> 183 us (0.65)
  waiting for transfers between devices: 139 us -> 41.1 us
  blocking collectives: 0 us -> 41.8 us
  Pallas kernels: 59.3 us -> 45.5 us
  between operations: 13.6 us -> 1.49 us
  matrix products: 11.9 us -> 0.51 us
  other arithmetic: 8.81 us -> 4.79 us
    all_to_all x3, waiting for transfers between devices: 106 us -> 28.4 us  [the longest x1 16.3 us: skewed(): lax.all_to_all(a, ('y', 'zh', 'zl'), 0, 0, tiled=True, axis_index_groups=...]
    all_to_all x0 -> x1, blocking collectives: none -> 41.8 us  [skewed(): lax.all_to_all(a, ('y', 'zh', 'zl'), 0, 0, tiled=True, axis_index_groups=...]
    pallas_call x1 -> x5, Pallas kernels: 59.3 us -> 45.5 us  [the longest x1 37.9 us: attention(): pl.pallas_call(attention_kernel, out_shape=jax.ShapeDtypeStruct((NX, ROWS...]
    all_gather x1 -> x0, waiting for transfers between devices: 12.1 us -> none  [local(): weight = lax.all_gather(out_weight, ('zl', 'core'), axis=0, tiled=True)]
    dot_general x1 -> x0, matrix products: 10.5 us -> none  [local(): proj = jnp.dot(attn, weight, preferred_element_type=jnp.float32)]
    ppermute x7 -> x4, waiting for transfers between devices: 18.6 us -> 8.63 us  [ring(): return lax.ppermute(a, axis, [((i + step) % 4, i) for i in range(4)])]
    mul x2 -> x0, local copies, waits for them, and re-layouts: 8.4 us -> none  [local(): attn = jnp.sum(part * share, axis=0).astype(jnp.bfloat16)]
    slice x1 -> x5, local copies, waits for them, and re-layouts: 0.02 us -> 5.33 us  [the longest x2 4.73 us: local(): w_2a, w_2b = (ring_z(w_p[:, :D // 2], 1), ring_z(w_m[:, D // 2:], 7))]
  transfers between devices with their start and end apart: 16 -> 18, of which waited for: 9 -> 8; matrix products, arithmetic and copies ran while one was open for 8% -> 6% of each run, Pallas kernels for 21% -> 23%
where the time goes in v2:
time: 183 us; the launch traced here: 180 us
  Pallas kernels  45.5 us (25%)
  blocking collectives  41.8 us (23%)
  waiting for transfers between devices  41.1 us (22%)
  starting transfers between devices  28.6 us (16%)
  local copies, waits for them, and re-layouts  16.6 us (9%)
  other arithmetic  4.79 us (3%)
    all_to_all x1, blocking collectives, skewed(): lax.all_to_all(a, ('y', 'zh', 'zl'), 0, 0, tiled=True, axis_index_groups=...  41.8 us
    pallas_call x1, Pallas kernels, attention(): pl.pallas_call(attention_kernel, out_shape=jax.ShapeDtypeStruct((NX, ROWS...  37.9 us
    all_to_all x1, waiting for transfers between devices, skewed(): lax.all_to_all(a, ('y', 'zh', 'zl'), 0, 0, tiled=True, axis_index_groups=...  16.3 us
    all_to_all x1, waiting for transfers between devices, local(): attn = combine(lax.all_to_all(sent, 'x', 0, 0, tiled=True))  12.2 us
    ppermute x4, waiting for transfers between devices, ring(): return lax.ppermute(a, axis, [((i + step) % 4, i) for i in range(4)])  8.63 us
    unnamed x28, local copies, waits for them, and re-layouts  7.59 us
    all_to_all x1, starting transfers between devices, skewed(): lax.all_to_all(a, ('y', 'zh', 'zl'), 0, 0, tiled=True, axis_index_groups=...  7.05 us
    all_to_all x1, starting transfers between devices, local(): attn = combine(lax.all_to_all(sent, 'x', 0, 0, tiled=True))  5.95 us
  transfers between devices with their start and end apart: 18, of which 8 were waited for; matrix products, arithmetic and copies ran while one was open for 6% of the time, Pallas kernels for 23%

profile of v2, /device:TPU:2, one launch (start us, length us, event | category | flops | bytes accessed | tf_op | source)
XLA Modules:
  0.0 180.3 jit_solution(1353518672478284734)
XLA Ops:
  0.0 1.1 copy.34
  1.1 1.2 bitcast_bitcast_fusion
  2.3 0.1 pad_maximum_fusion
  2.5 41.8 %all_to_all.20 = bf16[8,64,1152]{2,1,0:T(8,128)(2,1)S(1)} all-to-all(bf16[8,64,1152]{2,1,0:T(8,128)(2,1)S(1)} %pad_maximum_fusion), channel_id=1, replica_groups={{0,66,132,198,8,74,140,206},{64,130,196,6,72,138,204,14},{128,194,4,70,..., dimensions={0} | all-to-all | bytes 2359296 | tf_op jit(solution)/shard_map/all_to_all | solution.py:294
  44.3 0.9 collective-permute-start
  45.2 1.2 collective-permute-start.1
  46.5 0.5 slice.54
  47.0 1.3 broadcast_in_dim.18
  48.3 4.8 %all-to-all-start.1 = ((bf16[4,512,384]{2,1,0:T(8,128)(2,1)}), bf16[4,512,384]{2,1,0:T(8,128)(2,1)}, u32[]{:S(2)}, u32[]{:S(2)}) async-start(bf16[4,512,384]{2,1,0:T(8,128)(2,1)} %broadcast_in_dim.18), calls=%async_computation.1 | async-start | bytes 3145728 | tf_op jit(solution)/shard_map/all_to_all | solution.py:314
  54.4 7.4 %collective-permute-done.refs_2_ = bf16[512,768]{1,0:T(8,128)(2,1)S(1)} collective-permute-done((bf16[512,768]{1,0:T(8,128)(2,1)S(1)}, bf16[512,768]{1,0:T(8,128)(2,1)S(1)}, u32[]{:S(2)}, u32[]{:S(2)}) %collective-permute-start) | collective-permute-done | bytes 786464 | tf_op jit(solution)/shard_map/ppermute | solution.py:283
  61.8 1.6 collective-permute-start.2
  63.4 0.6 collective-permute-start.3
  64.0 0.2 copy-done.5
  64.3 3.3 %broadcast_select_fusion.refs_0_ = bf16[384,3072]{1,0:T(8,128)(2,1)} fusion(bf16[384,3072]{1,0:T(8,128)(2,1)} %param.12, pred[]{:T(512)} %bitcast.14), kind=kLoop, calls=%fused_computation | loop fusion | flops 1179648 | bytes 4718593 | tf_op jit(solution)/shard_map/jit(_where)/select_n | solution.py:316
  67.5 2.5 %collective-permute-start.10 = (bf16[384,3072]{1,0:T(8,128)(2,1)}, bf16[384,3072]{1,0:T(8,128)(2,1)S(1)}, u32[]{:S(2)}, u32[]{:S(2)}) collective-permute-start(bf16[384,3072]{1,0:T(8,128)(2,1)} %broadcast_select_fusion.refs_0_), channel_id=1, source_target_pairs={{2,0},{4,2},{6,4},{8,6},{10,8},{12,10},{14,12},{0,14},{3,1},{5,3},... | collective-permute-start | bytes 7077896 | tf_op jit(solution)/shard_map/ppermute | solution.py:298
  70.0 0.5 collective-permute-done.2.refs_4_
  70.6 0.7 copy-done.7
  71.3 0.5 collective-permute-start.5
  71.8 0.7 collective-permute-done.3.refs_5_
  72.6 0.8 copy-done.9
  73.4 0.5 collective-permute-start.8
  73.9 0.2 reduce-window.8
  74.1 0.1 pad_add_fusion.pos_ref
  74.2 1.6 collective-permute-done.8.refs_10_
  75.8 1.1 copy-done.4
  76.9 1.1 copy-done.6
  78.1 1.0 copy-done.8
  79.1 1.0 copy-done.10
  80.1 37.9 %attention.1.refs_0_ = bf16[4,544,384]{2,1,0:T(8,128)(2,1)} custom-call(s32[4]{0:T(128)S(1)} %bitcast.51, s32[4]{0:T(128)S(1)} %pad_add_fusion.pos_ref, bf16[4,512,384]{2,1,0:T(8,128)(2,1)} %all-to-all-done.1.refs_0_, bf16[512,768]{1,0:T(8,128)(2,1)S(1)} %slice.49.refs_1_, bf16[512,768]{1,0:T(8,128)(2,1)S(1)} %copy-done.4, bf16[512,768]{1,0:T(8,128)(2,1)S(1)} %copy-done.6, ...), custom_call_target="tpu_custom_call" | custom-call | flops 1000000 | bytes 1000000 | tf_op jit(solution)/shard_map/attention/pallas_call | solution.py:164
  118.0 6.0 %all-to-all-start.2 = ((bf16[4,544,384]{2,1,0:T(8,128)(2,1)}), bf16[4,544,384]{2,1,0:T(8,128)(2,1)}, u32[]{:S(2)}, u32[]{:S(2)}) async-start(bf16[4,544,384]{2,1,0:T(8,128)(2,1)} %attention.1.refs_0_), calls=%async_computation.2 | async-start | bytes 3342336 | tf_op jit(solution)/shard_map/all_to_all | solution.py:325
  123.9 1.4 copy-done.1
  125.4 2.4 %slice.44 = bf16[384,1536]{1,0:T(8,128)(2,1)} slice(bf16[384,3072]{1,0:T(8,128)(2,1)} %get-tuple-element.9.refs_1_), slice={[0:384], [0:1536]} | slice | bytes 2359296 | tf_op jit(solution)/shard_map/slice | solution.py:324
  127.7 2.7 %collective-permute-start.12 = (bf16[384,1536]{1,0:T(8,128)(2,1)}, bf16[384,1536]{1,0:T(8,128)(2,1)}, u32[]{:S(2)}, u32[]{:S(2)}) collective-permute-start(bf16[384,1536]{1,0:T(8,128)(2,1)} %slice.44), channel_id=1, source_target_pairs={{2,0},{4,2},{6,4},{8,6},{10,8},{12,10},{14,12},{0,14},{3,1},{5,3},... | collective-permute-start | bytes 3538952 | tf_op jit(solution)/shard_map/ppermute | solution.py:298
  130.4 2.4 %slice.45 = bf16[384,1536]{1,0:T(8,128)(2,1)} slice(bf16[384,3072]{1,0:T(8,128)(2,1)} %get-tuple-element.10.refs_2_), slice={[0:384], [1536:3072]} | slice | bytes 2359296 | tf_op jit(solution)/shard_map/slice | solution.py:324
  132.8 12.2 %all-to-all-done.2.got_ref = bf16[4,544,384]{2,1,0:T(8,128)(2,1)} async-done(((bf16[4,544,384]{2,1,0:T(8,128)(2,1)}), bf16[4,544,384]{2,1,0:T(8,128)(2,1)}, u32[]{:S(2)}, u32[]{:S(2)}) %all-to-all-start.2) | async-done | bytes 1671200 | tf_op jit(solution)/shard_map/all_to_all | solution.py:325
  145.0 3.3 %combine.1.refs_0_ = bf16[512,384]{1,0:T(8,128)(2,1)} custom-call(bf16[4,544,384]{2,1,0:T(8,128)(2,1)} %all-to-all-done.2.got_ref), custom_call_target="tpu_custom_call" | custom-call | flops 4000000 | bytes 2500000 | tf_op jit(solution)/shard_map/combine/pallas_call | solution.py:210
  148.2 7.0 %all-to-all-start.3 = ((bf16[8,64,384]{2,1,0:T(8,128)(2,1)}), bf16[8,64,384]{2,1,0:T(8,128)(2,1)S(1)}, u32[]{:S(2)}, u32[]{:S(2)}) async-start(bf16[8,64,384]{2,1,0:T(8,128)(2,1)} %bitcast.10), calls=%async_computation.3 | async-start | bytes 786432 | tf_op jit(solution)/shard_map/all_to_all | solution.py:294
  155.3 16.3 %all-to-all-done.3 = bf16[8,64,384]{2,1,0:T(8,128)(2,1)S(1)} async-done(((bf16[8,64,384]{2,1,0:T(8,128)(2,1)}), bf16[8,64,384]{2,1,0:T(8,128)(2,1)S(1)}, u32[]{:S(2)}, u32[]{:S(2)}) %all-to-all-start.3) | async-done | bytes 393248 | tf_op jit(solution)/shard_map/all_to_all | solution.py:294
  171.6 0.1 collective-permute-start.9
  171.7 1.4 collective-permute-done.9.got_ref
  173.1 0.1 copy-done.2
  173.2 4.3 %project.1 = bf16[2,64,3072]{2,1,0:T(8,128)(2,1)S(1)} custom-call(s32[4]{0:T(128)S(1)} %pad_add_fusion.pos_ref, bf16[4,64,384]{2,1,0:T(8,128)(2,1)S(1)} %get-tuple-element.14.keep_ref, bf16[4,64,384]{2,1,0:T(8,128)(2,1)S(1)} %collective-permute-done.9.got_ref, bf16[384,3072]{1,0:T(8,128)(2,1)} %broadcast_select_fusion.refs_0_, ...), custom_call_target="tpu_custom_call" | custom-call | flops 1207959552 | bytes 10000000 | tf_op jit(solution)/shard_map/project/pallas_call | solution.py:247
  177.5 0.1 collective-permute-start.14
  177.6 0.1 convert_reduce_fusion
  177.7 0.1 select_reduce_fusion
  177.8 0.5 fusion.3
  178.3 1.0 collective-permute-done.14
  179.4 0.9 fusion.2
  (43 shorter events, 0.3 us)
Async XLA Ops:
  0.0 177.8 %copy-start = (f32[8,3072]{1,0:T(8,128)S(1)}, f32[8,3072]{1,0:T(8,128)}, u32[]{:S(2)}) copy-start(f32[8,3072]{1,0:T(8,128)} %param.13) | copy-start | bytes 294916
  44.3 17.4 %collective-permute-start = (bf16[512,768]{1,0:T(8,128)(2,1)S(1)}, bf16[512,768]{1,0:T(8,128)(2,1)S(1)}, u32[]{:S(2)}, u32[]{:S(2)}) collective-permute-start(bf16[512,768]{1,0:T(8,128)(2,1)S(1)} %slice.49.refs_1_), channel_id=1, source_target_pairs={{64,0},{128,64},{192,128},{0,192},{65,1},{129,65},{193,129},{1,193... | collective-permute-start | bytes 2359304 | tf_op jit(solution)/shard_map/ppermute | solution.py:283
  45.2 18.2 %collective-permute-start.1 = (bf16[512,768]{1,0:T(8,128)(2,1)S(1)}, bf16[512,768]{1,0:T(8,128)(2,1)S(1)}, u32[]{:S(2)}, u32[]{:S(2)}) collective-permute-start(bf16[512,768]{1,0:T(8,128)(2,1)S(1)} %slice.49.refs_1_), channel_id=1, source_target_pairs={{192,0},{0,64},{64,128},{128,192},{193,1},{1,65},{65,129},{129,193... | collective-permute-start | bytes 2359304 | tf_op jit(solution)/shard_map/ppermute | solution.py:283
  46.4 24.9 %collective-permute-start.4 = (bf16[512,768]{1,0:T(8,128)(2,1)S(1)}, bf16[512,768]{1,0:T(8,128)(2,1)}, u32[]{:S(2)}, u32[]{:S(2)}) collective-permute-start(bf16[512,768]{1,0:T(8,128)(2,1)S(1)} %slice.49.refs_1_), channel_id=1, source_target_pairs={{0,1},{1,0},{2,3},{3,2},{4,5},{5,4},{6,7},{7,6},{8,9},{9,8},{10,11... | collective-permute-start | bytes 2359304 | tf_op jit(solution)/shard_map/ppermute | solution.py:287
  48.3 25.9 %all-to-all-start.1 = ((bf16[4,512,384]{2,1,0:T(8,128)(2,1)}), bf16[4,512,384]{2,1,0:T(8,128)(2,1)}, u32[]{:S(2)}, u32[]{:S(2)}) async-start(bf16[4,512,384]{2,1,0:T(8,128)(2,1)} %broadcast_in_dim.18), calls=%async_computation.1 | async-start | bytes 3145728 | tf_op jit(solution)/shard_map/all_to_all | solution.py:314
  61.8 2.3 %copy-start.3 = (bf16[512,768]{1,0:T(8,128)(2,1)}, bf16[512,768]{1,0:T(8,128)(2,1)S(1)}, u32[]{:S(2)}) copy-start(bf16[512,768]{1,0:T(8,128)(2,1)S(1)} %collective-permute-done.refs_2_) | copy-start | bytes 2359300
  61.8 8.8 %collective-permute-start.2 = (bf16[256,768]{1,0:T(8,128)(2,1)S(1)}, bf16[256,768]{1,0:T(8,128)(2,1)S(1)}, u32[]{:S(2)}, u32[]{:S(2)}) collective-permute-start(bf16[256,768]{1,0:T(8,128)(2,1)S(1)} %slice.50), channel_id=1, source_target_pairs={{64,0},{128,64},{192,128},{0,192},{65,1},{129,65},{193,129},{1,193... | collective-permute-start | bytes 1179656 | tf_op jit(solution)/shard_map/ppermute | solution.py:283
  63.4 0.9 copy-start.5
  63.4 9.2 %collective-permute-start.3 = (bf16[256,768]{1,0:T(8,128)(2,1)S(1)}, bf16[256,768]{1,0:T(8,128)(2,1)}, u32[]{:S(2)}, u32[]{:S(2)}) collective-permute-start(bf16[256,768]{1,0:T(8,128)(2,1)S(1)} %slice.51), channel_id=1, source_target_pairs={{192,0},{0,64},{64,128},{128,192},{193,1},{1,65},{65,129},{129,193... | collective-permute-start | bytes 1179656 | tf_op jit(solution)/shard_map/ppermute | solution.py:283
  64.3 9.6 %copy-start.12 = (s32[4]{0:T(128)S(1)}, s32[4]{0:T(128)}, u32[]{:S(2)}) copy-start(s32[4]{0:T(128)} %param.14) | copy-start | bytes 52
  67.5 56.4 %collective-permute-start.10 = (bf16[384,3072]{1,0:T(8,128)(2,1)}, bf16[384,3072]{1,0:T(8,128)(2,1)S(1)}, u32[]{:S(2)}, u32[]{:S(2)}) collective-permute-start(bf16[384,3072]{1,0:T(8,128)(2,1)} %broadcast_select_fusion.refs_0_), channel_id=1, source_target_pairs={{2,0},{4,2},{6,4},{8,6},{10,8},{12,10},{14,12},{0,14},{3,1},{5,3},... | collective-permute-start | bytes 7077896 | tf_op jit(solution)/shard_map/ppermute | solution.py:298
  70.0 53.9 %collective-permute-start.11 = (bf16[384,3072]{1,0:T(8,128)(2,1)}, bf16[384,3072]{1,0:T(8,128)(2,1)}, u32[]{:S(2)}, u32[]{:S(2)}) collective-permute-start(bf16[384,3072]{1,0:T(8,128)(2,1)} %broadcast_select_fusion.refs_0_), channel_id=1, source_target_pairs={{14,0},{0,2},{2,4},{4,6},{6,8},{8,10},{10,12},{12,14},{15,1},{1,3}... | collective-permute-start | bytes 7077896 | tf_op jit(solution)/shard_map/ppermute | solution.py:298
  70.6 2.0 %collective-permute-start.7 = (bf16[256,768]{1,0:T(8,128)(2,1)S(1)}, bf16[256,768]{1,0:T(8,128)(2,1)S(1)}, u32[]{:S(2)}, u32[]{:S(2)}) collective-permute-start(bf16[256,768]{1,0:T(8,128)(2,1)S(1)} %collective-permute-done.2.refs_4_), channel_id=1, source_target_pairs={{0,1},{1,0},{2,3},{3,2},{4,5},{5,4},{6,7},{7,6},{8,9},{9,8},{10,11... | collective-permute-start | bytes 1179656 | tf_op jit(solution)/shard_map/ppermute | solution.py:287
  70.6 0.7 copy-start.7
  71.3 4.5 %collective-permute-start.5 = (bf16[512,768]{1,0:T(8,128)(2,1)}, bf16[512,768]{1,0:T(8,128)(2,1)}, u32[]{:S(2)}, u32[]{:S(2)}) collective-permute-start(bf16[512,768]{1,0:T(8,128)(2,1)} %copy-done.3), channel_id=1, source_target_pairs={{0,1},{1,0},{2,3},{3,2},{4,5},{5,4},{6,7},{7,6},{8,9},{9,8},{10,11... | collective-permute-start | bytes 2359304 | tf_op jit(solution)/shard_map/ppermute | solution.py:287
  72.6 3.2 %collective-permute-start.6 = (bf16[512,768]{1,0:T(8,128)(2,1)}, bf16[512,768]{1,0:T(8,128)(2,1)}, u32[]{:S(2)}, u32[]{:S(2)}) collective-permute-start(bf16[512,768]{1,0:T(8,128)(2,1)} %copy-done.5), channel_id=1, source_target_pairs={{0,1},{1,0},{2,3},{3,2},{4,5},{5,4},{6,7},{7,6},{8,9},{9,8},{10,11... | collective-permute-start | bytes 2359304 | tf_op jit(solution)/shard_map/ppermute | solution.py:287
  72.6 0.8 copy-start.9
  73.4 2.4 %collective-permute-start.8 = (bf16[256,768]{1,0:T(8,128)(2,1)}, bf16[256,768]{1,0:T(8,128)(2,1)}, u32[]{:S(2)}, u32[]{:S(2)}) collective-permute-start(bf16[256,768]{1,0:T(8,128)(2,1)} %collective-permute-done.3.refs_5_), channel_id=1, source_target_pairs={{0,1},{1,0},{2,3},{3,2},{4,5},{5,4},{6,7},{7,6},{8,9},{9,8},{10,11... | collective-permute-start | bytes 1179656 | tf_op jit(solution)/shard_map/ppermute | solution.py:287
  75.8 1.1 copy-start.4
  76.9 1.1 copy-start.6
  78.1 1.0 copy-start.8
  79.1 1.0 copy-start.10
  118.0 27.0 %all-to-all-start.2 = ((bf16[4,544,384]{2,1,0:T(8,128)(2,1)}), bf16[4,544,384]{2,1,0:T(8,128)(2,1)}, u32[]{:S(2)}, u32[]{:S(2)}) async-start(bf16[4,544,384]{2,1,0:T(8,128)(2,1)} %attention.1.refs_0_), calls=%async_computation.2 | async-start | bytes 3342336 | tf_op jit(solution)/shard_map/all_to_all | solution.py:325
  123.9 1.5 copy-start.1
  127.7 44.0 %collective-permute-start.12 = (bf16[384,1536]{1,0:T(8,128)(2,1)}, bf16[384,1536]{1,0:T(8,128)(2,1)}, u32[]{:S(2)}, u32[]{:S(2)}) collective-permute-start(bf16[384,1536]{1,0:T(8,128)(2,1)} %slice.44), channel_id=1, source_target_pairs={{2,0},{4,2},{6,4},{8,6},{10,8},{12,10},{14,12},{0,14},{3,1},{5,3},... | collective-permute-start | bytes 3538952 | tf_op jit(solution)/shard_map/ppermute | solution.py:298
  132.8 38.9 %collective-permute-start.13 = (bf16[384,1536]{1,0:T(8,128)(2,1)}, bf16[384,1536]{1,0:T(8,128)(2,1)}, u32[]{:S(2)}, u32[]{:S(2)}) collective-permute-start(bf16[384,1536]{1,0:T(8,128)(2,1)} %slice.45), channel_id=1, source_target_pairs={{14,0},{0,2},{2,4},{4,6},{6,8},{8,10},{10,12},{12,14},{15,1},{1,3}... | collective-permute-start | bytes 3538952 | tf_op jit(solution)/shard_map/ppermute | solution.py:298
  148.2 23.3 %all-to-all-start.3 = ((bf16[8,64,384]{2,1,0:T(8,128)(2,1)}), bf16[8,64,384]{2,1,0:T(8,128)(2,1)S(1)}, u32[]{:S(2)}, u32[]{:S(2)}) async-start(bf16[8,64,384]{2,1,0:T(8,128)(2,1)} %bitcast.10), calls=%async_computation.3 | async-start | bytes 786432 | tf_op jit(solution)/shard_map/all_to_all | solution.py:294
  171.5 1.7 copy-start.2
  171.6 1.5 collective-permute-start.9
  173.2 4.5 %copy-start.13 = (s32[4]{0:T(128)S(1)}, s32[4]{0:T(128)}, u32[]{:S(2)}) copy-start(s32[4]{0:T(128)} %param.15) | copy-start | bytes 52
  177.5 1.9 %copy-start.11 = (bf16[64,3072]{1,0:T(8,128)(2,1)S(1)}, bf16[64,3072]{1,0:T(8,128)(2,1)}, u32[]{:S(2)}) copy-start(bf16[64,3072]{1,0:T(8,128)(2,1)} %param.11) | copy-start | bytes 1179652
  177.5 1.8 %collective-permute-start.14 = (bf16[64,3072]{1,0:T(8,128)(2,1)S(1)}, bf16[64,3072]{1,0:T(8,128)(2,1)S(1)}, u32[]{:S(2)}, u32[]{:S(2)}) collective-permute-start(bf16[64,3072]{1,0:T(8,128)(2,1)S(1)} %slice_bitcast_fusion), channel_id=1, source_target_pairs={{0,1},{1,0},{2,3},{3,2},{4,5},{5,4},{6,7},{7,6},{8,9},{9,8},{10,11... | collective-permute-start | bytes 1179656 | tf_op jit(solution)/shard_map/ppermute | solution.py:287

commit v3 on v2

--- a/solution.py
+++ b/solution.py
@@ -176,7 +176,7 @@
             pltpu.VMEM((NX, QROWS, HD), jnp.float32),
             pltpu.SemaphoreType.DMA((n_copies,)),
         ],
-        compiler_params=pltpu.CompilerParams(vmem_limit_bytes=48 * 1024 * 1024),
+        compiler_params=pltpu.CompilerParams(vmem_limit_bytes=58 * 1024 * 1024),
         cost_estimate=pl.CostEstimate(
             flops=1_000_000, bytes_accessed=1_000_000, transcendentals=1_000
         ),

time: 183 us -> 176 us (0.962)
  starting transfers between devices: 28.6 us -> 25.7 us
  local copies, waits for them, and re-layouts: 16.6 us -> 14 us
    unnamed x28 -> x26, local copies, waits for them, and re-layouts: 7.59 us -> 3.03 us
    ppermute x4, waiting for transfers between devices: 8.63 us -> 11.5 us  [ring(): return lax.ppermute(a, axis, [((i + step) % 4, i) for i in range(4)])]
    all_to_all x1, waiting for transfers between devices: 16.3 us -> 14.3 us  [skewed(): lax.all_to_all(a, ('y', 'zh', 'zl'), 0, 0, tiled=True, axis_index_groups=...]
  transfers between devices with their start and end apart: 18 -> 18, of which waited for: 8 -> 9; matrix products, arithmetic and copies ran while one was open for 6% -> 7% of each run, Pallas kernels for 23% -> 23%
where the time goes in v3:
time: 176 us; the launch traced here: 174 us
  Pallas kernels  44.2 us (25%)
  waiting for transfers between devices  42 us (24%)
  blocking collectives  41.8 us (24%)
  starting transfers between devices  25.7 us (15%)
  local copies, waits for them, and re-layouts  14 us (8%)
  other arithmetic  4.11 us (2%)
    all_to_all x1, blocking collectives, skewed(): lax.all_to_all(a, ('y', 'zh', 'zl'), 0, 0, tiled=True, axis_index_groups=...  41.8 us
    pallas_call x1, Pallas kernels, attention(): pl.pallas_call(attention_kernel, out_shape=jax.ShapeDtypeStruct((NX, ROWS...  36.7 us
    all_to_all x1, waiting for transfers between devices, skewed(): lax.all_to_all(a, ('y', 'zh', 'zl'), 0, 0, tiled=True, axis_index_groups=...  14.3 us
    all_to_all x1, waiting for transfers between devices, local(): attn = combine(lax.all_to_all(sent, 'x', 0, 0, tiled=True))  12.3 us
    ppermute x4, waiting for transfers between devices, ring(): return lax.ppermute(a, axis, [((i + step) % 4, i) for i in range(4)])  11.5 us
    all_to_all x1, starting transfers between devices, skewed(): lax.all_to_all(a, ('y', 'zh', 'zl'), 0, 0, tiled=True, axis_index_groups=...  6.18 us
    all_to_all x1, starting transfers between devices, local(): lax.all_to_all(jnp.broadcast_to(q[None], (NX, QROWS, W)), 'x', 0, 0, tile...  4.96 us
    all_to_all x1, starting transfers between devices, local(): attn = combine(lax.all_to_all(sent, 'x', 0, 0, tiled=True))  4.91 us
  transfers between devices with their start and end apart: 18, of which 9 were waited for; matrix products, arithmetic and copies ran while one was open for 7% of the time, Pallas kernels for 23%

profile of v3, /device:TPU:2, one launch (start us, length us, event | category | flops | bytes accessed | tf_op | source)
XLA Modules:
  0.0 173.8 jit_solution(10660566862112617474)
XLA Ops:
  0.0 1.1 copy.34
  1.1 1.2 bitcast_bitcast_fusion
  2.3 0.1 pad_maximum_fusion
  2.5 41.8 %all_to_all.20 = bf16[8,64,1152]{2,1,0:T(8,128)(2,1)S(1)} all-to-all(bf16[8,64,1152]{2,1,0:T(8,128)(2,1)S(1)} %pad_maximum_fusion), channel_id=1, replica_groups={{0,66,132,198,8,74,140,206},{64,130,196,6,72,138,204,14},{128,194,4,70,..., dimensions={0} | all-to-all | bytes 2359296 | tf_op jit(solution)/shard_map/all_to_all | solution.py:294
  44.3 0.1 slice.49.refs_1_
  44.3 0.9 collective-permute-start
  45.2 1.2 collective-permute-start.1
  46.5 0.5 slice.54
  47.0 1.3 broadcast_in_dim.18
  48.3 5.0 %all-to-all-start.1 = ((bf16[4,512,384]{2,1,0:T(8,128)(2,1)}), bf16[4,512,384]{2,1,0:T(8,128)(2,1)}, u32[]{:S(2)}, u32[]{:S(2)}) async-start(bf16[4,512,384]{2,1,0:T(8,128)(2,1)} %broadcast_in_dim.18), calls=%async_computation.1 | async-start | bytes 3145728 | tf_op jit(solution)/shard_map/all_to_all | solution.py:314
  54.6 7.3 %collective-permute-done.refs_2_ = bf16[512,768]{1,0:T(8,128)(2,1)} collective-permute-done((bf16[512,768]{1,0:T(8,128)(2,1)S(1)}, bf16[512,768]{1,0:T(8,128)(2,1)}, u32[]{:S(2)}, u32[]{:S(2)}) %collective-permute-start) | collective-permute-done | bytes 786464 | tf_op jit(solution)/shard_map/ppermute | solution.py:283
  61.9 1.0 slice.50
  62.9 1.6 collective-permute-start.2
  64.5 1.0 slice.51
  65.5 0.6 collective-permute-start.3
  66.1 1.6 broadcast_select_fusion.refs_0_
  67.7 2.0 %collective-permute-start.10 = (bf16[384,3072]{1,0:T(8,128)(2,1)}, bf16[384,3072]{1,0:T(8,128)(2,1)S(1)}, u32[]{:S(2)}, u32[]{:S(2)}) collective-permute-start(bf16[384,3072]{1,0:T(8,128)(2,1)} %broadcast_select_fusion.refs_0_), channel_id=1, source_target_pairs={{2,0},{4,2},{6,4},{8,6},{10,8},{12,10},{14,12},{0,14},{3,1},{5,3},... | collective-permute-start | bytes 7077896 | tf_op jit(solution)/shard_map/ppermute | solution.py:298
  69.8 1.8 %collective-permute-done.2.refs_4_ = bf16[256,768]{1,0:T(8,128)(2,1)S(1)} collective-permute-done((bf16[256,768]{1,0:T(8,128)(2,1)S(1)}, bf16[256,768]{1,0:T(8,128)(2,1)S(1)}, u32[]{:S(2)}, u32[]{:S(2)}) %collective-permute-start.2) | collective-permute-done | bytes 393248 | tf_op jit(solution)/shard_map/ppermute | solution.py:283
  71.6 0.7 copy-done.7
  72.3 2.3 %collective-permute-done.3.refs_5_ = bf16[256,768]{1,0:T(8,128)(2,1)} collective-permute-done((bf16[256,768]{1,0:T(8,128)(2,1)S(1)}, bf16[256,768]{1,0:T(8,128)(2,1)}, u32[]{:S(2)}, u32[]{:S(2)}) %collective-permute-start.3) | collective-permute-done | bytes 393248 | tf_op jit(solution)/shard_map/ppermute | solution.py:283
  74.7 0.7 copy-done.8
  75.4 0.5 collective-permute-start.8
  75.9 0.7 reduce-window.8
  76.6 0.6 pad_add_fusion.pos_ref
  77.2 0.7 collective-permute-done.8.refs_10_
  77.9 0.9 copy-done.6
  78.8 36.7 %attention.1.refs_0_ = bf16[4,544,384]{2,1,0:T(8,128)(2,1)} custom-call(s32[4]{0:T(128)} %bitcast.59, s32[4]{0:T(128)} %pad_add_fusion.pos_ref, bf16[4,512,384]{2,1,0:T(8,128)(2,1)} %all-to-all-done.1.refs_0_, bf16[512,768]{1,0:T(8,128)(2,1)} %copy-done.4, bf16[512,768]{1,0:T(8,128)(2,1)} %collective-permute-done.refs_2_, ...), custom_call_target="tpu_custom_call" | custom-call | flops 1000000 | bytes 1000000 | tf_op jit(solution)/shard_map/attention/pallas_call | solution.py:164
  115.5 4.9 %all-to-all-start.2 = ((bf16[4,544,384]{2,1,0:T(8,128)(2,1)}), bf16[4,544,384]{2,1,0:T(8,128)(2,1)}, u32[]{:S(2)}, u32[]{:S(2)}) async-start(bf16[4,544,384]{2,1,0:T(8,128)(2,1)} %attention.1.refs_0_), calls=%async_computation.2 | async-start | bytes 3342336 | tf_op jit(solution)/shard_map/all_to_all | solution.py:325
  120.4 0.9 collective-permute-done.11.refs_2_
  121.3 0.5 copy-done.1
  121.8 2.4 %slice.44 = bf16[384,1536]{1,0:T(8,128)(2,1)} slice(bf16[384,3072]{1,0:T(8,128)(2,1)} %get-tuple-element.9.refs_1_), slice={[0:384], [0:1536]} | slice | bytes 2359296 | tf_op jit(solution)/shard_map/slice | solution.py:324
  124.2 2.5 %collective-permute-start.12 = (bf16[384,1536]{1,0:T(8,128)(2,1)}, bf16[384,1536]{1,0:T(8,128)(2,1)}, u32[]{:S(2)}, u32[]{:S(2)}) collective-permute-start(bf16[384,1536]{1,0:T(8,128)(2,1)} %slice.44), channel_id=1, source_target_pairs={{2,0},{4,2},{6,4},{8,6},{10,8},{12,10},{14,12},{0,14},{3,1},{5,3},... | collective-permute-start | bytes 3538952 | tf_op jit(solution)/shard_map/ppermute | solution.py:298
  126.7 2.4 %slice.45 = bf16[384,1536]{1,0:T(8,128)(2,1)} slice(bf16[384,3072]{1,0:T(8,128)(2,1)} %get-tuple-element.10.refs_2_), slice={[0:384], [1536:3072]} | slice | bytes 2359296 | tf_op jit(solution)/shard_map/slice | solution.py:324
  129.1 12.3 %all-to-all-done.2.got_ref = bf16[4,544,384]{2,1,0:T(8,128)(2,1)} async-done(((bf16[4,544,384]{2,1,0:T(8,128)(2,1)}), bf16[4,544,384]{2,1,0:T(8,128)(2,1)}, u32[]{:S(2)}, u32[]{:S(2)}) %all-to-all-start.2) | async-done | bytes 1671200 | tf_op jit(solution)/shard_map/all_to_all | solution.py:325
  141.4 3.3 %combine.1.refs_0_ = bf16[512,384]{1,0:T(8,128)(2,1)} custom-call(bf16[4,544,384]{2,1,0:T(8,128)(2,1)} %all-to-all-done.2.got_ref), custom_call_target="tpu_custom_call" | custom-call | flops 4000000 | bytes 2500000 | tf_op jit(solution)/shard_map/combine/pallas_call | solution.py:210
  144.6 6.2 %all-to-all-start.3 = ((bf16[8,64,384]{2,1,0:T(8,128)(2,1)}), bf16[8,64,384]{2,1,0:T(8,128)(2,1)S(1)}, u32[]{:S(2)}, u32[]{:S(2)}) async-start(bf16[8,64,384]{2,1,0:T(8,128)(2,1)} %bitcast.10), calls=%async_computation.3 | async-start | bytes 786432 | tf_op jit(solution)/shard_map/all_to_all | solution.py:294
  150.8 14.3 %all-to-all-done.3 = bf16[8,64,384]{2,1,0:T(8,128)(2,1)S(1)} async-done(((bf16[8,64,384]{2,1,0:T(8,128)(2,1)}), bf16[8,64,384]{2,1,0:T(8,128)(2,1)S(1)}, u32[]{:S(2)}, u32[]{:S(2)}) %all-to-all-start.3) | async-done | bytes 393248 | tf_op jit(solution)/shard_map/all_to_all | solution.py:294
  165.2 0.1 collective-permute-start.9
  165.3 1.4 collective-permute-done.9.got_ref
  166.7 0.1 copy-done.2
  166.8 4.2 %project.1 = bf16[2,64,3072]{2,1,0:T(8,128)(2,1)S(1)} custom-call(s32[4]{0:T(128)S(1)} %copy-done.3, bf16[4,64,384]{2,1,0:T(8,128)(2,1)S(1)} %get-tuple-element.14.keep_ref, bf16[4,64,384]{2,1,0:T(8,128)(2,1)S(1)} %collective-permute-done.9.got_ref, bf16[384,3072]{1,0:T(8,128)(2,1)} %broadcast_select_fusion.refs_0_, bf16[384,3072]{1,0:T(8,128)(2,1)S(1)} %copy-done.2, ...), custom_call_target="tpu_custom_call" | custom-call | flops 1207959552 | bytes 10000000 | tf_op jit(solution)/shard_map/project/pallas_call | solution.py:247
  171.0 0.0 copy-start.9
  171.1 0.2 collective-permute-start.14
  171.2 0.1 convert_reduce_fusion
  171.3 0.1 select_reduce_fusion
  171.4 0.5 fusion.3
  171.9 1.0 collective-permute-done.14
  172.9 0.9 fusion.2
  (41 shorter events, 0.2 us)
Async XLA Ops:
  0.0 171.4 %copy-start = (f32[8,3072]{1,0:T(8,128)S(1)}, f32[8,3072]{1,0:T(8,128)}, u32[]{:S(2)}) copy-start(f32[8,3072]{1,0:T(8,128)} %param.13) | copy-start | bytes 294916
  44.3 4.0 %copy-start.4 = (bf16[512,768]{1,0:T(8,128)(2,1)}, bf16[512,768]{1,0:T(8,128)(2,1)S(1)}, u32[]{:S(2)}) copy-start(bf16[512,768]{1,0:T(8,128)(2,1)S(1)} %slice.49.refs_1_) | copy-start | bytes 2359300
  44.3 17.5 %collective-permute-start = (bf16[512,768]{1,0:T(8,128)(2,1)S(1)}, bf16[512,768]{1,0:T(8,128)(2,1)}, u32[]{:S(2)}, u32[]{:S(2)}) collective-permute-start(bf16[512,768]{1,0:T(8,128)(2,1)S(1)} %slice.49.refs_1_), channel_id=1, source_target_pairs={{64,0},{128,64},{192,128},{0,192},{65,1},{129,65},{193,129},{1,193... | collective-permute-start | bytes 2359304 | tf_op jit(solution)/shard_map/ppermute | solution.py:283
  45.2 19.3 %collective-permute-start.1 = (bf16[512,768]{1,0:T(8,128)(2,1)S(1)}, bf16[512,768]{1,0:T(8,128)(2,1)}, u32[]{:S(2)}, u32[]{:S(2)}) collective-permute-start(bf16[512,768]{1,0:T(8,128)(2,1)S(1)} %slice.49.refs_1_), channel_id=1, source_target_pairs={{192,0},{0,64},{64,128},{128,192},{193,1},{1,65},{65,129},{129,193... | collective-permute-start | bytes 2359304 | tf_op jit(solution)/shard_map/ppermute | solution.py:283
  46.4 25.2 %collective-permute-start.4 = (bf16[512,768]{1,0:T(8,128)(2,1)S(1)}, bf16[512,768]{1,0:T(8,128)(2,1)}, u32[]{:S(2)}, u32[]{:S(2)}) collective-permute-start(bf16[512,768]{1,0:T(8,128)(2,1)S(1)} %slice.49.refs_1_), channel_id=1, source_target_pairs={{0,1},{1,0},{2,3},{3,2},{4,5},{5,4},{6,7},{7,6},{8,9},{9,8},{10,11... | collective-permute-start | bytes 2359304 | tf_op jit(solution)/shard_map/ppermute | solution.py:287
  48.3 17.8 %copy-start.5 = (bf16[384,3072]{1,0:T(8,128)(2,1)S(1)}, bf16[384,3072]{1,0:T(8,128)(2,1)}, u32[]{:S(2)}) copy-start(bf16[384,3072]{1,0:T(8,128)(2,1)} %param.12) | copy-start | bytes 7077892
  48.3 28.9 %all-to-all-start.1 = ((bf16[4,512,384]{2,1,0:T(8,128)(2,1)}), bf16[4,512,384]{2,1,0:T(8,128)(2,1)}, u32[]{:S(2)}, u32[]{:S(2)}) async-start(bf16[4,512,384]{2,1,0:T(8,128)(2,1)} %broadcast_in_dim.18), calls=%async_computation.1 | async-start | bytes 3145728 | tf_op jit(solution)/shard_map/all_to_all | solution.py:314
  62.9 8.7 %collective-permute-start.2 = (bf16[256,768]{1,0:T(8,128)(2,1)S(1)}, bf16[256,768]{1,0:T(8,128)(2,1)S(1)}, u32[]{:S(2)}, u32[]{:S(2)}) collective-permute-start(bf16[256,768]{1,0:T(8,128)(2,1)S(1)} %slice.50), channel_id=1, source_target_pairs={{64,0},{128,64},{192,128},{0,192},{65,1},{129,65},{193,129},{1,193... | collective-permute-start | bytes 1179656 | tf_op jit(solution)/shard_map/ppermute | solution.py:283
  65.5 9.2 %collective-permute-start.3 = (bf16[256,768]{1,0:T(8,128)(2,1)S(1)}, bf16[256,768]{1,0:T(8,128)(2,1)}, u32[]{:S(2)}, u32[]{:S(2)}) collective-permute-start(bf16[256,768]{1,0:T(8,128)(2,1)S(1)} %slice.51), channel_id=1, source_target_pairs={{192,0},{0,64},{64,128},{128,192},{193,1},{1,65},{65,129},{129,193... | collective-permute-start | bytes 1179656 | tf_op jit(solution)/shard_map/ppermute | solution.py:283
  66.1 9.8 %copy-start.11 = (s32[4]{0:T(128)S(1)}, s32[4]{0:T(128)}, u32[]{:S(2)}) copy-start(s32[4]{0:T(128)} %param.14) | copy-start | bytes 52
  67.7 52.7 %collective-permute-start.10 = (bf16[384,3072]{1,0:T(8,128)(2,1)}, bf16[384,3072]{1,0:T(8,128)(2,1)S(1)}, u32[]{:S(2)}, u32[]{:S(2)}) collective-permute-start(bf16[384,3072]{1,0:T(8,128)(2,1)} %broadcast_select_fusion.refs_0_), channel_id=1, source_target_pairs={{2,0},{4,2},{6,4},{8,6},{10,8},{12,10},{14,12},{0,14},{3,1},{5,3},... | collective-permute-start | bytes 7077896 | tf_op jit(solution)/shard_map/ppermute | solution.py:298
  69.7 51.5 %collective-permute-start.11 = (bf16[384,3072]{1,0:T(8,128)(2,1)}, bf16[384,3072]{1,0:T(8,128)(2,1)}, u32[]{:S(2)}, u32[]{:S(2)}) collective-permute-start(bf16[384,3072]{1,0:T(8,128)(2,1)} %broadcast_select_fusion.refs_0_), channel_id=1, source_target_pairs={{14,0},{0,2},{2,4},{4,6},{6,8},{8,10},{10,12},{12,14},{15,1},{1,3}... | collective-permute-start | bytes 7077896 | tf_op jit(solution)/shard_map/ppermute | solution.py:298
  71.6 0.7 copy-start.7
  71.6 3.1 %collective-permute-start.7 = (bf16[256,768]{1,0:T(8,128)(2,1)S(1)}, bf16[256,768]{1,0:T(8,128)(2,1)S(1)}, u32[]{:S(2)}, u32[]{:S(2)}) collective-permute-start(bf16[256,768]{1,0:T(8,128)(2,1)S(1)} %collective-permute-done.2.refs_4_), channel_id=1, source_target_pairs={{0,1},{1,0},{2,3},{3,2},{4,5},{5,4},{6,7},{7,6},{8,9},{9,8},{10,11... | collective-permute-start | bytes 1179656 | tf_op jit(solution)/shard_map/ppermute | solution.py:287
  72.3 5.5 %collective-permute-start.5 = (bf16[512,768]{1,0:T(8,128)(2,1)}, bf16[512,768]{1,0:T(8,128)(2,1)S(1)}, u32[]{:S(2)}, u32[]{:S(2)}) collective-permute-start(bf16[512,768]{1,0:T(8,128)(2,1)} %collective-permute-done.refs_2_), channel_id=1, source_target_pairs={{0,1},{1,0},{2,3},{3,2},{4,5},{5,4},{6,7},{7,6},{8,9},{9,8},{10,11... | collective-permute-start | bytes 2359304 | tf_op jit(solution)/shard_map/ppermute | solution.py:287
  74.7 3.2 %collective-permute-start.6 = (bf16[512,768]{1,0:T(8,128)(2,1)}, bf16[512,768]{1,0:T(8,128)(2,1)}, u32[]{:S(2)}, u32[]{:S(2)}) collective-permute-start(bf16[512,768]{1,0:T(8,128)(2,1)} %collective-permute-done.1.refs_3_), channel_id=1, source_target_pairs={{0,1},{1,0},{2,3},{3,2},{4,5},{5,4},{6,7},{7,6},{8,9},{9,8},{10,11... | collective-permute-start | bytes 2359304 | tf_op jit(solution)/shard_map/ppermute | solution.py:287
  74.7 0.7 copy-start.8
  75.4 2.4 %collective-permute-start.8 = (bf16[256,768]{1,0:T(8,128)(2,1)}, bf16[256,768]{1,0:T(8,128)(2,1)}, u32[]{:S(2)}, u32[]{:S(2)}) collective-permute-start(bf16[256,768]{1,0:T(8,128)(2,1)} %collective-permute-done.3.refs_5_), channel_id=1, source_target_pairs={{0,1},{1,0},{2,3},{3,2},{4,5},{5,4},{6,7},{7,6},{8,9},{9,8},{10,11... | collective-permute-start | bytes 1179656 | tf_op jit(solution)/shard_map/ppermute | solution.py:287
  77.9 0.9 copy-start.6
  115.5 25.9 %all-to-all-start.2 = ((bf16[4,544,384]{2,1,0:T(8,128)(2,1)}), bf16[4,544,384]{2,1,0:T(8,128)(2,1)}, u32[]{:S(2)}, u32[]{:S(2)}) async-start(bf16[4,544,384]{2,1,0:T(8,128)(2,1)} %attention.1.refs_0_), calls=%async_computation.2 | async-start | bytes 3342336 | tf_op jit(solution)/shard_map/all_to_all | solution.py:325
  120.4 1.4 copy-start.1
  124.2 41.1 %collective-permute-start.12 = (bf16[384,1536]{1,0:T(8,128)(2,1)}, bf16[384,1536]{1,0:T(8,128)(2,1)}, u32[]{:S(2)}, u32[]{:S(2)}) collective-permute-start(bf16[384,1536]{1,0:T(8,128)(2,1)} %slice.44), channel_id=1, source_target_pairs={{2,0},{4,2},{6,4},{8,6},{10,8},{12,10},{14,12},{0,14},{3,1},{5,3},... | collective-permute-start | bytes 3538952 | tf_op jit(solution)/shard_map/ppermute | solution.py:298
  129.1 36.2 %collective-permute-start.13 = (bf16[384,1536]{1,0:T(8,128)(2,1)}, bf16[384,1536]{1,0:T(8,128)(2,1)}, u32[]{:S(2)}, u32[]{:S(2)}) collective-permute-start(bf16[384,1536]{1,0:T(8,128)(2,1)} %slice.45), channel_id=1, source_target_pairs={{14,0},{0,2},{2,4},{4,6},{6,8},{8,10},{10,12},{12,14},{15,1},{1,3}... | collective-permute-start | bytes 3538952 | tf_op jit(solution)/shard_map/ppermute | solution.py:298
  144.6 20.5 %all-to-all-start.3 = ((bf16[8,64,384]{2,1,0:T(8,128)(2,1)}), bf16[8,64,384]{2,1,0:T(8,128)(2,1)S(1)}, u32[]{:S(2)}, u32[]{:S(2)}) async-start(bf16[8,64,384]{2,1,0:T(8,128)(2,1)} %bitcast.10), calls=%async_computation.3 | async-start | bytes 786432 | tf_op jit(solution)/shard_map/all_to_all | solution.py:294
  165.1 1.7 copy-start.2
  165.1 1.7 copy-start.3
  165.2 1.5 collective-permute-start.9
  166.8 4.4 %copy-start.10 = (s32[4,1]{0,1:T(1,128)S(1)}, s32[4,1]{0,1:T(1,128)}, u32[]{:S(2)}) copy-start(s32[4,1]{0,1:T(1,128)} %reduce-window.8) | copy-start | bytes 52
  166.8 4.5 %copy-start.12 = (s32[4]{0:T(128)S(1)}, s32[4]{0:T(128)}, u32[]{:S(2)}) copy-start(s32[4]{0:T(128)} %param.15) | copy-start | bytes 52
  171.0 1.9 %copy-start.9 = (bf16[64,3072]{1,0:T(8,128)(2,1)S(1)}, bf16[64,3072]{1,0:T(8,128)(2,1)}, u32[]{:S(2)}) copy-start(bf16[64,3072]{1,0:T(8,128)(2,1)} %param.11) | copy-start | bytes 1179652
  171.1 1.8 %collective-permute-start.14 = (bf16[64,3072]{1,0:T(8,128)(2,1)S(1)}, bf16[64,3072]{1,0:T(8,128)(2,1)S(1)}, u32[]{:S(2)}, u32[]{:S(2)}) collective-permute-start(bf16[64,3072]{1,0:T(8,128)(2,1)S(1)} %slice_bitcast_fusion), channel_id=1, source_target_pairs={{0,1},{1,0},{2,3},{3,2},{4,5},{5,4},{6,7},{7,6},{8,9},{9,8},{10,11... | collective-permute-start | bytes 1179656 | tf_op jit(solution)/shard_map/ppermute | solution.py:287
